TPU v7x, 128 devices: a whole 4x4x4 slice. The times are simulated.
128 devices in a mesh: grp: 4 (over y_lo, core), slab: 32 (over z, x, y_hi).
Axes of the slice: x: 4, y: 4 (y_hi: 2, y_lo: 2; y = y_hi * 2 + y_lo), z: 4, core: 2. Of those that a mesh axis runs over, the one named last changes fastest.
Arguments:
- modes: bfloat16 [512, 2, 384, 384], P(('grp', 'slab')), may hold values from -0.21875 to 0.21875
- occup: float32 [512, 384], P(('grp', 'slab')), may hold values from 0.2 to 5
- qprime_coord: int32 [3, 512], P(None, ('grp', 'slab')), may hold values from 0 to 15
- shell_vec: int32 [3, 128], replicated, may hold values from -3 to 3
- target_coord: int32 [3, 128], replicated, may hold values from 0 to 15
- pair_atoms: int32 [2, 1024], replicated, may hold values from 0 to 127
- block_in: int32 [2097152], P(('grp', 'slab')), may hold values from 0 to 4095
- block_out: int32 [2097152], P(('grp', 'slab')), may hold values from 0 to 4095
- fc4: bfloat16 [81, 2097152], P(None, ('grp', 'slab')), may hold values from -0.29882812 to 0.29882812
Outputs:
- delta: float32 [128, 2, 9, 1024], P(('grp', 'slab'))
All inputs are finite; a program needn't handle non-finite values.
Results may differ from a plain program's by a relative error of at most 0.0024.
Values sent between devices are 32-bit elements; how exact they have to be, the bound alone decides.
No kernel may reach another device: no remote copies, remote signals or barrier semaphores. Data moves between devices by JAX's collectives and lax.ppermute only.
A program may use at most 256 MiB of HBM per device.

v0:
```python
import math

import jax
import jax.numpy as jnp
from jax import lax
from jax.sharding import PartitionSpec as P

MESH = 16


def phases(coords, shells):
    wave_index = jnp.mod(jnp.sum(coords[:, :, None] * shells[:, None, :], axis=0), MESH)
    angle = 2.0 * math.pi / MESH * wave_index.astype(jnp.float32)
    return (jnp.cos(angle), jnp.sin(angle))


def pair_density(mode_pair, weights, atom_first, atom_second):
    real_part = mode_pair[0]
    imag_part = mode_pair[1]
    left_rows = jnp.concatenate([real_part, imag_part], 1)
    doubled = jnp.concatenate([weights, weights])
    scaled = (left_rows.astype(jnp.float32) * doubled[None, :]).astype(jnp.bfloat16)
    right_rows = jnp.concatenate([left_rows, jnp.concatenate([imag_part, -real_part], 1)], 0)
    density = jnp.dot(right_rows, scaled.T, preferred_element_type=jnp.float32)
    natoms = real_part.shape[0] // 3
    blocked = density.reshape(2, natoms, 3, natoms, 3).transpose(1, 3, 0, 2, 4)
    picked = blocked[atom_first, atom_second]
    return picked.reshape(atom_first.shape[0], 2, 9).transpose(1, 2, 0)


def contract_blocks(own_rows, fc4, block_in, block_out):
    entries = own_rows.shape[1]
    low_width = 128
    high_width = entries // low_width
    table = own_rows.reshape(9, high_width, low_width)
    nblocks = fc4.shape[1]
    step_size = min(4096, nblocks)
    nsteps = nblocks // step_size
    coeff_steps = fc4.reshape(81, nsteps, step_size).transpose(1, 0, 2)
    read_steps = block_in.reshape(nsteps, step_size)
    write_steps = block_out.reshape(nsteps, step_size)
    low_iota = lax.broadcasted_iota(jnp.int32, (1, low_width), 1)
    high_iota = lax.broadcasted_iota(jnp.int32, (1, high_width), 1)

    def one_step(carry, inputs):
        coeffs, reads, writes = inputs
        read_low = (reads[:, None] % low_width == low_iota).astype(jnp.float32)
        read_high = (reads[:, None] // low_width == high_iota).astype(jnp.float32)
        partly = jnp.einsum("jab,kb->jak", table, read_low, precision=lax.Precision.HIGHEST)
        gathered = jnp.sum(partly * read_high.T[None], axis=1)
        contrib = jnp.sum(
            coeffs.reshape(9, 9, step_size).astype(jnp.float32) * gathered[None], axis=1
        )
        write_low = (writes[:, None] % low_width == low_iota).astype(jnp.float32)
        write_high = (writes[:, None] // low_width == high_iota).astype(jnp.float32)
        spread = contrib[:, None, :] * write_high.T[None]
        carry = carry + jnp.einsum(
            "jhk,kl->jhl", spread, write_low, precision=lax.Precision.HIGHEST
        )
        return (carry, None)

    start = jnp.zeros((9, high_width, low_width), jnp.float32)
    result = lax.scan(one_step, start, (coeff_steps, read_steps, write_steps))[0]
    return result.reshape(9, entries)


def shards(
    modes, occup, qprime_coord, shell_vec, target_coord, pair_atoms, block_in, block_out, fc4
):
    npairs = pair_atoms.shape[1]
    nshells = shell_vec.shape[1]
    local_points = modes.shape[0]
    nslab = lax.axis_size("slab")
    ngroups = lax.axis_size("grp")
    ndevices = nslab * ngroups
    per_slab = nshells // nslab
    atom_first = pair_atoms[0]
    atom_second = pair_atoms[1]
    pieces = lax.map(
        lambda inputs: pair_density(inputs[0], inputs[1], atom_first, atom_second), (modes, occup)
    )
    stacked = pieces.reshape(local_points, 2, 9 * npairs)
    cos_prime, sin_prime = phases(qprime_coord, shell_vec)
    partial_value = jnp.dot(cos_prime.T, stacked[:, 0], precision=lax.Precision.HIGHEST)
    partial_value = partial_value - jnp.dot(
        sin_prime.T, stacked[:, 1], precision=lax.Precision.HIGHEST
    )
    partial_value = (partial_value / math.sqrt(local_points * ndevices)).reshape(nshells, 9, npairs)
    summed = lax.psum(partial_value, ("grp", "slab"))
    own_rho = lax.dynamic_slice_in_dim(summed, lax.axis_index("slab") * per_slab, per_slab, 0)
    own_rows = own_rho.transpose(1, 0, 2).reshape(9, per_slab * npairs)
    own_renorm = contract_blocks(own_rows, fc4, block_in, block_out)
    own_shells = own_renorm.reshape(9, per_slab, npairs).transpose(1, 0, 2)
    renorm = jnp.zeros((nshells, 9, npairs), jnp.float32)
    renorm = lax.dynamic_update_slice_in_dim(
        renorm, own_shells, lax.axis_index("slab") * per_slab, 0
    )
    cos_target, sin_target = phases(target_coord, shell_vec)
    ntarget = target_coord.shape[1]
    own_targets = ntarget // ndevices
    total_renorm = lax.psum(renorm, ("grp", "slab"))
    total_rows = total_renorm.reshape(nshells, 9 * npairs)
    first_row = lax.axis_index(("grp", "slab")) * own_targets
    cos_rows = lax.dynamic_slice_in_dim(cos_target, first_row, own_targets, 0)
    sin_rows = lax.dynamic_slice_in_dim(sin_target, first_row, own_targets, 0)
    real_out = jnp.dot(cos_rows, total_rows, precision=lax.Precision.HIGHEST)
    imag_out = -jnp.dot(sin_rows, total_rows, precision=lax.Precision.HIGHEST)
    delta = jnp.stack([real_out, imag_out], 1).reshape(own_targets, 2, 9, npairs)
    return delta


def solution(mesh):
    return jax.shard_map(
        shards,
        mesh=mesh,
        in_specs=(
            P(("grp", "slab"), None, None, None),
            P(("grp", "slab"), None),
            P(None, ("grp", "slab")),
            P(),
            P(),
            P(),
            P(("grp", "slab")),
            P(("grp", "slab")),
            P(None, ("grp", "slab")),
        ),
        out_specs=P(("grp", "slab"), None, None, None),
        check_vma=False,
    )
```

profile of v0, /device:TPU:1, one launch (start us, length us, event | category | flops | bytes accessed | tf_op | source)
XLA Modules:
  0.0 1053.2 jit_solution(4037808429007012555)
XLA Ops:
  7.3 604.9 %while.25 = (s32[]{:T(128)}, f32[4,2,9,1024]{3,1,2,0:T(2,128)S(1)}, bf16[4,2,384,384]{3,2,1,0:T(8,128)(2,1)}, f32[4,384]{1,0:T(4,128)}, s32[1024]{0:T(1024)S(1)}...) while((s32[]{:T(128)}, f32[4,2,9,1024]{3,1,2,0:T(2,128)S(1)}, bf16[4,2,384,384]{3,2,1,0:T(8,128)(2,1)}, ...), condition=%wide.region_3.4_spmd, body=%wide.region_2.3_spmd.sunk | while | flops 459632384 | bytes 8731261 | solution.py:79
  10.9 49.0 %reshape.385 = f32[2,128,3,128,3]{4,3,2,1,0:T(8,128)} reshape(f32[768,384]{1,0:T(8,128)S(1)} %fusion.89) | data formatting | bytes 2359296 | tf_op jit(solution)/shard_map/while/body/eval_jaxpr/reshape | solution.py:26
  59.9 81.8 %copy.50 = f32[2,128,3,128,3]{4,0,2,3,1:T(2,128)} copy(f32[2,128,3,128,3]{4,3,2,1,0:T(8,128)} %reshape.385) | data formatting | bytes 2359296 | tf_op jit(solution)/shard_map/while/body/eval_jaxpr/reshape | solution.py:26
  141.7 14.6 %gather_fusion = f32[1024,2,3,3]{3,1,2,0:T(2,128)S(1)} fusion(f32[128,128,2,3,3]{4,2,3,1,0:T(2,128)} %bitcast.95, s32[1024]{0:T(1024)S(1)} %bitcast.94), kind=kCustom, calls=%fused_computation.clone.1 | custom fusion | bytes 155648 | tf_op jit(solution)/shard_map/while/body/eval_jaxpr/gather | solution.py:27
  156.3 2.3 copy.51
  162.2 49.0 %reshape.385 = f32[2,128,3,128,3]{4,3,2,1,0:T(8,128)} reshape(f32[768,384]{1,0:T(8,128)S(1)} %fusion.89) | data formatting | bytes 2359296 | tf_op jit(solution)/shard_map/while/body/eval_jaxpr/reshape | solution.py:26
  211.1 81.8 %copy.50 = f32[2,128,3,128,3]{4,0,2,3,1:T(2,128)} copy(f32[2,128,3,128,3]{4,3,2,1,0:T(8,128)} %reshape.385) | data formatting | bytes 2359296 | tf_op jit(solution)/shard_map/while/body/eval_jaxpr/reshape | solution.py:26
  292.9 14.6 %gather_fusion = f32[1024,2,3,3]{3,1,2,0:T(2,128)S(1)} fusion(f32[128,128,2,3,3]{4,2,3,1,0:T(2,128)} %bitcast.95, s32[1024]{0:T(1024)S(1)} %bitcast.94), kind=kCustom, calls=%fused_computation.clone.1 | custom fusion | bytes 155648 | tf_op jit(solution)/shard_map/while/body/eval_jaxpr/gather | solution.py:27
  307.5 2.3 copy.51
  313.4 49.0 %reshape.385 = f32[2,128,3,128,3]{4,3,2,1,0:T(8,128)} reshape(f32[768,384]{1,0:T(8,128)S(1)} %fusion.89) | data formatting | bytes 2359296 | tf_op jit(solution)/shard_map/while/body/eval_jaxpr/reshape | solution.py:26
  362.4 81.8 %copy.50 = f32[2,128,3,128,3]{4,0,2,3,1:T(2,128)} copy(f32[2,128,3,128,3]{4,3,2,1,0:T(8,128)} %reshape.385) | data formatting | bytes 2359296 | tf_op jit(solution)/shard_map/while/body/eval_jaxpr/reshape | solution.py:26
  444.2 14.6 %gather_fusion = f32[1024,2,3,3]{3,1,2,0:T(2,128)S(1)} fusion(f32[128,128,2,3,3]{4,2,3,1,0:T(2,128)} %bitcast.95, s32[1024]{0:T(1024)S(1)} %bitcast.94), kind=kCustom, calls=%fused_computation.clone.1 | custom fusion | bytes 155648 | tf_op jit(solution)/shard_map/while/body/eval_jaxpr/gather | solution.py:27
  458.8 2.3 copy.51
  464.6 49.0 %reshape.385 = f32[2,128,3,128,3]{4,3,2,1,0:T(8,128)} reshape(f32[768,384]{1,0:T(8,128)S(1)} %fusion.89) | data formatting | bytes 2359296 | tf_op jit(solution)/shard_map/while/body/eval_jaxpr/reshape | solution.py:26
  513.6 81.8 %copy.50 = f32[2,128,3,128,3]{4,0,2,3,1:T(2,128)} copy(f32[2,128,3,128,3]{4,3,2,1,0:T(8,128)} %reshape.385) | data formatting | bytes 2359296 | tf_op jit(solution)/shard_map/while/body/eval_jaxpr/reshape | solution.py:26
  595.4 14.6 %gather_fusion = f32[1024,2,3,3]{3,1,2,0:T(2,128)S(1)} fusion(f32[128,128,2,3,3]{4,2,3,1,0:T(2,128)} %bitcast.95, s32[1024]{0:T(1024)S(1)} %bitcast.94), kind=kCustom, calls=%fused_computation.clone.1 | custom fusion | bytes 155648 | tf_op jit(solution)/shard_map/while/body/eval_jaxpr/gather | solution.py:27
  610.0 2.3 copy.51
  612.6 4.0 fusion.50
  616.6 5.9 fusion.47
  622.5 6.1 copy.28
  628.9 1.5 copy-done.2
  630.4 3.0 reshape.356
  633.5 3.3 copy.30
  636.8 150.5 %all-reduce.3.cloned.1.call-done = f32[128,9,1024]{0,2,1:T(8,128)} async-done(((f32[128,9,1024]{0,2,1:T(8,128)}), f32[128,9,1024]{0,2,1:T(8,128)}) %all-reduce.3.cloned.1.call-update) | async-done | bytes 4718608 | tf_op jit(solution)/shard_map/psum | solution.py:89
  787.3 5.8 dynamic-slice_bitcast_fusion.2
  793.1 3.1 copy.29
  796.9 49.6 %while.26 = (s32[]{:T(128)}, f32[9,32,128]{2,1,0:T(8,128)}, bf16[4,81,4096]{2,1,0:T(8,128)(2,1)S(1)}, s32[4,4096]{1,0:T(4,128)S(1)}, f32[9,32,128]{2,1,0:T(8,128...) while((s32[]{:T(128)}, f32[9,32,128]{2,1,0:T(8,128)}, ...), condition=%wide.region_8.9_spmd.clone.clone, body=%wide.region_5.8_spmd.clone.clone.sunk | while | flops 3630141440 | bytes 30564512 | solution.py:63
  797.0 3.8 fusion.97
  800.8 1.3 dynamic-slice_convert_fusion.2
  802.0 1.5 reshape.386
  804.8 4.4 fusion.98
  809.4 3.8 fusion.97
  813.1 1.3 dynamic-slice_convert_fusion.2
  814.4 1.5 reshape.386
  817.2 4.5 fusion.98
  821.8 3.8 fusion.97
  825.6 1.3 dynamic-slice_convert_fusion.2
  826.8 1.5 reshape.386
  829.6 4.5 fusion.98
  834.2 3.8 fusion.97
  839.2 1.5 reshape.386
  842.0 4.5 fusion.98
  847.4 2.9 copy.31
  850.3 2.5 broadcast_in_dim.17
  852.8 22.7 %dynamic_update_slice.7 = f32[128,9,1024]{0,2,1:T(8,128)} dynamic-update-slice(f32[128,9,1024]{0,2,1:T(8,128)} %broadcast_in_dim.17, f32[4,9,1024]{0,2,1:T(8,128)} %copy.31, s32[]{:T(128)S(6)} %select_n.100, s32[]{:T(128)} %constant.139.clone.1, s32[]{:T(128)} %constant.139.clone.1) | dynamic-update-slice | bytes 294916 | tf_op jit(solution)/shard_map/dynamic_update_slice | solution.py:95
  876.4 156.7 %all-reduce.5.cloned.1.call-done = f32[128,9216]{0,1:T(8,128)} async-done(((f32[128,9216]{0,1:T(8,128)}), f32[128,9216]{0,1:T(8,128)}) %all-reduce.5.cloned.1.call-update) | async-done | bytes 4718608 | tf_op jit(solution)/shard_map/psum | solution.py:101
  1033.1 6.2 fusion.63
  1039.4 6.2 fusion.61
  (102 shorter events, 25.7 us)
Async XLA Ops:
  6.5 780.8 %all-reduce.3.cloned.1.call-start = ((), (), s32[]{:S(2)}) async-start(), calls=%async_computation | async-start | bytes 9437184 | tf_op jit(solution)/shard_map/psum | solution.py:89
  7.3 605.2 %copy-start.5 = (s32[3,128]{1,0:T(4,128)S(1)}, s32[3,128]{1,0:T(4,128)}, u32[]{:S(2)}) copy-start(s32[3,128]{1,0:T(4,128)} %param.16) | copy-start | bytes 4612
  7.3 605.2 %copy-start.7 = (s32[3,4]{1,0:T(4,128)S(1)}, s32[3,4]{1,0:T(4,128)}, u32[]{:S(2)}) copy-start(s32[3,4]{1,0:T(4,128)} %param.15) | copy-start | bytes 148
  628.6 1.8 copy-start.2
  628.6 404.5 %all-reduce.5.cloned.1.call-start = ((), (), s32[]{:S(2)}) async-start(), calls=%async_computation.1 | async-start | bytes 9437184 | tf_op jit(solution)/shard_map/psum | solution.py:101
  633.5 3.3 copy-start.3
  633.5 3.3 copy-start.4
  796.9 3.9 copy-start
  804.8 4.5 copy-start.1
  809.3 3.9 copy-start
  817.1 4.5 copy-start.1
  821.7 3.9 copy-start
  829.5 4.5 copy-start.1
  834.1 3.9 copy-start
  841.9 4.5 copy-start.1
  875.5 0.7 copy-start.6
  875.5 0.7 copy-start.8
Sparse Core Ops, SparseCore 0:
  628.8 158.4 all-reduce.2
  875.7 157.3 all-reduce.4
where the time goes:
time: 1060 us; the launch traced here: 1050 us
  local copies, waits for them, and re-layouts  659 us (62%)
  waiting for transfers between devices  307 us (29%)
  matrix products  58.4 us (6%)
  other arithmetic  14.7 us (1%)
  between operations  13.6 us (1%)
    reshape x8, local copies, waits for them, and re-layouts, pair_density(): blocked = density.reshape(2, natoms, 3, natoms, 3).transpose(1, 3, 0, 2, 4)  523 us
    psum x1, waiting for transfers between devices, shards(): total_renorm = lax.psum(renorm, ('grp', 'slab'))  157 us
    psum x1, waiting for transfers between devices, shards(): summed = lax.psum(partial_value, ('grp', 'slab'))  150 us
    gather x8, local copies, waits for them, and re-layouts, pair_density(): picked = blocked[atom_first, atom_second]  67.4 us
    dynamic_update_slice x1, local copies, waits for them, and re-layouts, shards(): lax.dynamic_update_slice_in_dim(renorm, own_shells, lax.axis_index('slab'...  22.7 us
  transfers between devices with their start and end apart: 2, of which 2 were waited for; matrix products, arithmetic and copies ran while one was open for 1% of the time, Pallas kernels for 0%

commit v1 on v0

v1 whole, which is shorter than its diff:
```python
import math

import jax
import jax.numpy as jnp
import numpy as np
from jax import lax
from jax.experimental import pallas as pl
from jax.experimental.pallas import tpu as pltpu
from jax.sharding import PartitionSpec as P

MESH = 16
LANES = 128
NDEV = 128
NPH = 8
COLS = 72
MSG = 75
ALL = ("grp", "slab")
F32 = jnp.float32
BF16 = jnp.bfloat16
HIGHEST = lax.Precision.HIGHEST
VMEM_LIMIT = 48 * 1024 * 1024


def params():
    return pltpu.CompilerParams(vmem_limit_bytes=VMEM_LIMIT)


def sixteenth_cos(index):
    wrapped = index - 16.0 * jnp.floor(index * (1.0 / 16.0))
    folded = 4.0 - jnp.minimum(wrapped, 16.0 - wrapped)
    square = folded * folded
    poly = POLY[3]
    for coefficient in (POLY[2], POLY[1], POLY[0]):
        poly = poly * square + coefficient
    return folded * poly


def odd_polynomial():
    points = np.arange(1, 5, dtype=np.float64)
    values = np.sin(np.pi * points / 8.0)
    powers = np.stack([points ** (2 * k + 1) for k in range(4)], 1)
    return [float(c) for c in np.linalg.solve(powers, values)]


POLY = odd_polynomial()


def pick_body(
    coord, atoms, modes, occup, out, held, weights, pairs, spots, points, scaled, rows, dens, sems
):
    copies = [
        pltpu.make_async_copy(occup, weights, sems.at[4]),
        pltpu.make_async_copy(atoms, pairs, sems.at[5]),
        pltpu.make_async_copy(coord, points, sems.at[6]),
    ]
    loads = [pltpu.make_async_copy(modes.at[q], held.at[q], sems.at[q]) for q in range(4)]
    loads[0].start()
    for copy in copies:
        copy.start()
    for load in loads[1:]:
        load.start()
    copies[1].wait()
    first = pairs[0:1, :]
    second = pairs[1:2, :]
    turn = (128 - 3 * (first & 31)) & 127
    pairs[0:1, :] = ((first >> 5) * 3072 + second * 24) * 128 + turn
    move = pltpu.make_async_copy(pairs.at[0], spots, sems.at[7])
    move.start()
    copies[0].wait()
    for q in range(4):
        loads[q].wait()
        weight = weights[q : q + 1, :]
        for part in range(2):
            values = held[q, part]
            span = pl.ds(384 * part, 384)
            scaled[:, span] = (values.astype(F32) * weight).astype(BF16)
            for block in range(4):
                piece = values[96 * block : 96 * block + 96]
                rows[128 * block : 128 * block + 96, span] = piece
                other = piece if part == 1 else -piece
                low = 512 + 128 * block
                rows[low : low + 96, pl.ds(384 * (1 - part), 384)] = other
        for comp in range(2):
            for half in range(2):
                start = 512 * comp + 256 * half
                tile = lax.dot_general(
                    scaled[...],
                    rows[start : start + 256],
                    (((1,), (1,)), ((), ())),
                    preferred_element_type=F32,
                )
                for low in range(2):
                    base = 3072 * (2 * half + low) + 2 * q + comp
                    dens[pl.ds(base, 384, stride=8), :] = tile[:, 128 * low : 128 * low + 128]

    lane = lax.broadcasted_iota(jnp.int32, (8, LANES), 1)
    row = lax.broadcasted_iota(jnp.int32, (8, LANES), 0)
    copies[2].wait()
    move.wait()
    start = jnp.zeros((8, LANES), F32)
    for q in range(4):
        for axis in range(3):
            here = (row // 2 == q) & (lane == COLS + axis)
            start = jnp.where(here, points[axis, q].astype(F32), start)

    def one(dev, carry):
        acc = start
        for high in range(NPH):
            spot = spots[high * LANES + dev]
            base = spot >> 7
            for beta in range(3):
                low = 24 * beta + 3 * high
                value = dens[pl.ds(pl.multiple_of(base + 8 * beta, 8), 8), :]
                turned = pltpu.roll(value, (spot + low) & 127, 1)
                acc = jnp.where((lane >= low) & (lane < low + 3), turned, acc)
        out[dev] = acc[:, :MSG]
        return carry

    lax.fori_loop(0, NDEV, one, 0, unroll=16)


def pick(modes, occup, coord, atoms):
    anywhere = pl.BlockSpec(memory_space=pl.ANY)
    return pl.pallas_call(
        pick_body,
        in_specs=[anywhere] * 4,
        out_specs=pl.BlockSpec(memory_space=pltpu.VMEM),
        out_shape=jax.ShapeDtypeStruct((NDEV, 8, MSG), F32),
        scratch_shapes=[
            pltpu.VMEM((4, 2, 384, 384), BF16),
            pltpu.VMEM((4, 384), F32),
            pltpu.VMEM((2, NPH * LANES), jnp.int32),
            pltpu.SMEM((NPH * LANES,), jnp.int32),
            pltpu.SMEM((3, 4), jnp.int32),
            pltpu.VMEM((384, 768), BF16),
            pltpu.VMEM((1024, 768), BF16),
            pltpu.VMEM((4 * 384 * 8, LANES), F32),
            pltpu.SemaphoreType.DMA((8,)),
        ],
        compiler_params=params(),
    )(coord, atoms, modes, occup)


def shells_body(received, shell, out):
    values = received[...].reshape(NDEV * 8, MSG)
    vectors = jnp.concatenate([jnp.zeros((COLS, LANES), F32), shell[...].astype(F32)], 0)
    index = lax.dot_general(
        vectors, values, (((0,), (1,)), ((), ())), preferred_element_type=F32
    )
    lane = lax.broadcasted_iota(jnp.int32, index.shape, 1)
    index = index + jnp.where(lane % 2 == 1, 4.0, 0.0)
    rho = jnp.dot(sixteenth_cos(index), values, precision=HIGHEST, preferred_element_type=F32)
    rho = rho[:, :COLS] * (1.0 / math.sqrt(512.0))
    for slab in range(32):
        piece = rho[4 * slab : 4 * slab + 4]
        for group in range(4):
            out[32 * group + slab] = piece


def to_shells(received, shell):
    return pl.pallas_call(
        shells_body,
        out_shape=jax.ShapeDtypeStruct((NDEV, 4, COLS), F32),
        compiler_params=params(),
    )(received, shell)


def block_tables():
    row = np.arange(2 * COLS)
    column = row % COLS
    beta, high, alpha = column // 24, (column % 24) // 3, column % 3
    comp = 3 * alpha + beta
    level = 8 * (row // COLS) + high
    term = np.arange(81)
    repeat = (term[:, None] % 9 == comp[None, :]).astype(np.float32)
    collect = (comp[:, None] == term[None, :] // 9).astype(np.float32)
    return repeat, collect, level.astype(np.int32)[:, None]


def contract_body(chunk, unroll, received, repeat, collect, level, reads, writes, fc4, out, table, total):
    for shell in range(4):
        piece = received[:, shell, :]
        piece = jnp.concatenate([piece, jnp.zeros((NDEV, LANES - COLS), F32)], 1)
        low, high = shell % 2, shell // 2
        table[low * COLS : low * COLS + COLS, high * LANES : high * LANES + LANES] = piece.T[
            :COLS
        ].astype(BF16)
    total[...] = jnp.zeros_like(total)
    place = lax.broadcasted_iota(jnp.int32, (2 * LANES, chunk), 0)

    def split(entry):
        low = ((entry >> 11) << 7) | (entry & 127)
        return jnp.where(place == low, 1.0, 0.0).astype(BF16), (entry >> 7) & 15

    def one(step, carry):
        span = pl.ds(pl.multiple_of(step * chunk, chunk), chunk)
        read_low, read_high = split(reads[:, span])
        write_low, write_high = split(writes[:, span])
        found = jnp.dot(table[...], read_low, preferred_element_type=F32)
        found = jnp.where(level[...] == read_high, found, 0.0).astype(BF16)
        spread = jnp.dot(repeat[...], found, preferred_element_type=F32)
        product = fc4[:, span].astype(F32) * spread
        coarse = product.astype(BF16)
        fine = (product - coarse.astype(F32)).astype(BF16)
        contrib = jnp.dot(collect[...], coarse, preferred_element_type=F32)
        contrib = contrib + jnp.dot(collect[...], fine, preferred_element_type=F32)
        contrib = jnp.where(level[...] == write_high, contrib, 0.0)
        coarse = contrib.astype(BF16)
        fine = (contrib - coarse.astype(F32)).astype(BF16)
        total[...] += lax.dot_general(
            jnp.concatenate([coarse, fine], 0),
            write_low,
            (((1,), (1,)), ((), ())),
            preferred_element_type=F32,
        )
        return carry

    lax.fori_loop(0, fc4.shape[1] // chunk, one, 0, unroll=unroll)
    for shell in range(4):
        low, high = shell % 2, shell // 2
        span = pl.ds(high * LANES, LANES)
        piece = total[low * COLS : low * COLS + COLS, span]
        piece = piece + total[(2 + low) * COLS : (2 + low) * COLS + COLS, span]
        piece = jnp.concatenate([piece, jnp.zeros((LANES - COLS, LANES), F32)], 0)
        out[:, shell, :] = piece.T[:, :COLS]


def contract(received, block_in, block_out, fc4, chunk=8192, unroll=1):
    nblocks = fc4.shape[1]
    repeat, collect, level = block_tables()

    def body(*refs):
        contract_body(chunk, unroll, *refs)

    return pl.pallas_call(
        body,
        out_shape=jax.ShapeDtypeStruct((NDEV, 4, COLS), F32),
        scratch_shapes=[
            pltpu.VMEM((2 * COLS, 2 * LANES), BF16),
            pltpu.VMEM((4 * COLS, 2 * LANES), F32),
        ],
        compiler_params=params(),
    )(
        received,
        jnp.asarray(repeat, BF16),
        jnp.asarray(collect, BF16),
        jnp.asarray(level),
        block_in.reshape(1, nblocks),
        block_out.reshape(1, nblocks),
        fc4,
    )


def targets_body(received, shell, target, out):
    rows = []
    for low in range(4):
        piece = received[:, low, :]
        rows.append(piece[0:32] + piece[32:64] + piece[64:96] + piece[96:128])
    renorm = jnp.concatenate(rows, 0)
    source = lax.broadcasted_iota(jnp.int32, (LANES, LANES), 0)
    order = lax.broadcasted_iota(jnp.int32, (LANES, LANES), 1)
    order = jnp.where(source == (order % 32) * 4 + order // 32, 1.0, 0.0)
    pad = jnp.zeros((5, LANES), F32)
    vectors = jnp.concatenate([shell[...].astype(F32), pad], 0)
    points = jnp.concatenate([target[...].astype(F32), pad], 0)
    vectors = jnp.dot(vectors, order, preferred_element_type=F32)
    index = lax.dot_general(
        points, vectors, (((0,), (0,)), ((), ())), preferred_element_type=F32
    )
    out[:, 0, :] = jnp.dot(
        sixteenth_cos(index), renorm, precision=HIGHEST, preferred_element_type=F32
    )
    out[:, 1, :] = jnp.dot(
        sixteenth_cos(index + 4.0), renorm, precision=HIGHEST, preferred_element_type=F32
    )


def to_targets(received, shell, target):
    return pl.pallas_call(
        targets_body,
        out_shape=jax.ShapeDtypeStruct((NDEV, 2, COLS), F32),
        compiler_params=params(),
    )(received, shell, target)


def arrange_body(received, out, turned):
    for comp in range(2):
        piece = received[:, comp, :]
        piece = jnp.concatenate([piece, jnp.zeros((NDEV, LANES - COLS), F32)], 1)
        turned[...] = piece.T
        for high in range(NPH):
            for alpha in range(3):
                out[0, 3 * alpha : 3 * alpha + 3, comp, LANES * high : LANES * high + LANES] = turned[
                    pl.ds(3 * high + alpha, 3, stride=24), :
                ]


def arrange(received):
    return pl.pallas_call(
        arrange_body,
        out_shape=jax.ShapeDtypeStruct((1, 9, 2, NPH * NDEV), F32),
        scratch_shapes=[pltpu.VMEM((LANES, LANES), F32)],
        compiler_params=params(),
    )(received)


def exchange(values):
    return lax.all_to_all(values, ALL, 0, 0, tiled=True)


def shards(
    modes, occup, qprime_coord, shell_vec, target_coord, pair_atoms, block_in, block_out, fc4
):
    picked = exchange(pick(modes, occup, qprime_coord, pair_atoms))
    density = exchange(to_shells(picked, shell_vec))
    renorm = exchange(contract(density, block_in, block_out, fc4))
    delta = exchange(to_targets(renorm, shell_vec, target_coord))
    return arrange(delta).transpose(0, 2, 1, 3)


def solution(mesh):
    return jax.shard_map(
        shards,
        mesh=mesh,
        in_specs=(
            P(("grp", "slab"), None, None, None),
            P(("grp", "slab"), None),
            P(None, ("grp", "slab")),
            P(),
            P(),
            P(),
            P(("grp", "slab")),
            P(("grp", "slab")),
            P(None, ("grp", "slab")),
        ),
        out_specs=P(("grp", "slab"), None, None, None),
        check_vma=False,
    )
```

time: 1060 us -> 95.1 us (0.09)
  local copies, waits for them, and re-layouts: 659 us -> 3.92 us
  waiting for transfers between devices: 307 us -> 0 us
  blocking collectives: 0 us -> 70.4 us
  matrix products: 58.4 us -> 0 us
  Pallas kernels: 0 us -> 20.4 us
  other arithmetic: 14.7 us -> 0 us
  between operations: 13.6 us -> 0.09 us
    reshape x11 -> x0, local copies, waits for them, and re-layouts: 526 us -> none  [the longest x8 523 us: pair_density(): blocked = density.reshape(2, natoms, 3, natoms, 3).transpose(1, 3, 0, 2, 4)]
    psum x2 -> x0, waiting for transfers between devices: 307 us -> none  [the longest x1 157 us: shards(): total_renorm = lax.psum(renorm, ('grp', 'slab'))]
    all_to_all x0 -> x4, blocking collectives: none -> 70.4 us  [exchange(): return lax.all_to_all(values, ALL, 0, 0, tiled=True)]
    gather x8 -> x0, local copies, waits for them, and re-layouts: 67.4 us -> none  [pair_density(): picked = blocked[atom_first, atom_second]]
    dot_general x16 -> x0, matrix products: 58.4 us -> none  [the longest x4 17.8 us: one_step(): jnp.einsum('jhk,kl->jhl', spread, write_low, precision=lax.Precision.HIGH...]
    dynamic_update_slice x5 -> x0, local copies, waits for them, and re-layouts: 22.8 us -> none  [the longest x1 22.7 us: shards(): lax.dynamic_update_slice_in_dim(renorm, own_shells, lax.axis_index('slab'...]
    pallas_call x0 -> x5, Pallas kernels: none -> 20.4 us  [the longest x1 9.23 us: contract(): pl.pallas_call(body, out_shape=jax.ShapeDtypeStruct((NDEV, 4, COLS), F32)...]
    transpose x3 -> x0, local copies, waits for them, and re-layouts: 11.8 us -> none  [the longest x2 8.86 us: shards(): own_rows = own_rho.transpose(1, 0, 2).reshape(9, per_slab * npairs)]
  transfers between devices with their start and end apart: 2 -> 0, of which waited for: 2 -> 0; matrix products, arithmetic and copies ran while one was open for 1% -> 0% of each run, Pallas kernels for 0% -> 0%
where the time goes in v1:
time: 95.1 us; the launch traced here: 94.8 us
  blocking collectives  70.4 us (74%)
  Pallas kernels  20.4 us (21%)
  local copies, waits for them, and re-layouts  3.92 us (4%)
    all_to_all x4, blocking collectives, exchange(): return lax.all_to_all(values, ALL, 0, 0, tiled=True)  70.4 us
    pallas_call x1, Pallas kernels, contract(): pl.pallas_call(body, out_shape=jax.ShapeDtypeStruct((NDEV, 4, COLS), F32)...  9.23 us
    pallas_call x1, Pallas kernels, pick(): pl.pallas_call(pick_body, in_specs=[anywhere] * 4, out_specs=pl.BlockSpec...  8.73 us
    unnamed x24, local copies, waits for them, and re-layouts  3.92 us

profile of v1, /device:TPU:1, one launch (start us, length us, event | category | flops | bytes accessed | tf_op | source)
XLA Modules:
  0.0 94.8 jit_solution(2183626029199901150)
XLA Ops:
  0.0 0.0 copy-start
  0.0 0.0 copy-start.1
  0.0 1.8 %copy-done.1 = bf16[4,2,384,384]{3,2,1,0:T(8,128)(2,1)S(1)} copy-done((bf16[4,2,384,384]{3,2,1,0:T(8,128)(2,1)S(1)}, bf16[4,2,384,384]{3,2,1,0:T(8,128)(2,1)}, u32[]{:S(2)}) %copy-start.1) | copy-done | bytes 2359320
  1.8 0.0 copy-start.7
  1.8 0.7 copy-done.7
  2.5 0.0 copy-start.9
  2.5 0.7 copy-done.9
  3.2 0.0 copy-start.11
  3.2 0.7 copy-done.11
  3.9 0.0 copy-start.8
  3.9 0.0 copy-start.2
  3.9 0.0 copy-start.3
  3.9 0.0 copy-start.4
  3.9 0.0 copy-start.5
  3.9 0.0 copy-start.6
  3.9 8.7 %shard_map.118 = f32[128,8,75]{2,1,0:T(8,128)S(1)} custom-call(s32[3,4]{1,0:T(4,128)S(1)} %copy-done.11, s32[2,1024]{1,0:T(2,128)S(1)} %copy-done.7, bf16[4,2,384,384]{3,2,1,0:T(8,128)(2,1)S(1)} %copy-done.1, f32[4,384]{1,0:T(4,128)S(1)} %copy-done.9), custom_call_target="tpu_custom_call" | custom-call | tf_op jit(solution)/shard_map/pallas_call | solution.py:124
  12.7 25.2 %all_to_all.20.received = f32[128,8,75]{2,1,0:T(8,128)S(1)} all-to-all(f32[128,8,75]{2,1,0:T(8,128)S(1)} %shard_map.118), channel_id=1, replica_groups=mesh['grp'=4,'slab'=32] {'grp','slab'}, dimensions={0} | all-to-all | bytes 614400 | tf_op jit(solution)/shard_map/all_to_all | solution.py:308
  37.9 0.0 copy-done.8
  37.9 0.0 copy-start.10
  37.9 1.0 %shard_map.119 = f32[128,4,72]{2,1,0:T(4,128)S(1)} custom-call(f32[128,8,75]{2,1,0:T(8,128)S(1)} %all_to_all.20.received, s32[3,128]{1,0:T(4,128)S(1)} %copy-done.8), custom_call_target="tpu_custom_call" | custom-call | tf_op jit(solution)/shard_map/pallas_call | solution.py:161
  38.9 15.4 %all_to_all.21.refs_0_ = f32[128,4,72]{2,1,0:T(4,128)S(1)} all-to-all(f32[128,4,72]{2,1,0:T(4,128)S(1)} %shard_map.119), channel_id=1, replica_groups=mesh['grp'=4,'slab'=32] {'grp','slab'}, dimensions={0} | all-to-all | bytes 294912 | tf_op jit(solution)/shard_map/all_to_all | solution.py:308
  54.3 0.0 copy-done
  54.3 0.0 copy-done.2
  54.3 0.0 copy-done.3
  54.3 0.0 copy-done.4
  54.3 0.0 copy-done.5
  54.3 0.0 copy-done.6
  54.3 9.2 %shard_map.120 = f32[128,4,72]{2,1,0:T(4,128)S(1)} custom-call(f32[128,4,72]{2,1,0:T(4,128)S(1)} %all_to_all.21.refs_0_, bf16[81,144]{1,0:T(8,128)(2,1)S(1)} %copy-done.5, bf16[144,81]{1,0:T(8,128)(2,1)S(1)} %copy-done.6, s32[144,1]{1,0:T(8,128)S(1)} %copy-done.2, s32[1,16384]{1,0:T(1,128)S(1)} %bitcast.3, s32[1,16384]{1,0:T(1,128)S(1)} %bitcast.4, ...), custom_call_target="tpu_custom_call" | custom-call | tf_op jit(solution)/shard_map/pallas_call | solution.py:235
  63.5 15.4 %all_to_all.22.received = f32[128,4,72]{2,1,0:T(4,128)S(1)} all-to-all(f32[128,4,72]{2,1,0:T(4,128)S(1)} %shard_map.120), channel_id=1, replica_groups=mesh['grp'=4,'slab'=32] {'grp','slab'}, dimensions={0} | all-to-all | bytes 294912 | tf_op jit(solution)/shard_map/all_to_all | solution.py:308
  78.9 0.0 copy-done.10
  78.9 0.7 shard_map.121
  79.6 14.4 %all_to_all.23.received = f32[128,2,72]{2,1,0:T(2,128)S(1)} all-to-all(f32[128,2,72]{2,1,0:T(2,128)S(1)} %shard_map.121), channel_id=1, replica_groups=mesh['grp'=4,'slab'=32] {'grp','slab'}, dimensions={0} | all-to-all | bytes 147456 | tf_op jit(solution)/shard_map/all_to_all | solution.py:308
  94.0 0.8 shard_map.122
Async XLA Ops:
  0.0 54.3 %copy-start = (bf16[81,16384]{1,0:T(8,128)(2,1)S(1)}, bf16[81,16384]{1,0:T(8,128)(2,1)}, u32[]{:S(2)}) copy-start(bf16[81,16384]{1,0:T(8,128)(2,1)} %refs_6_.1) | copy-start | bytes 7962628
  0.0 1.8 %copy-start.1 = (bf16[4,2,384,384]{3,2,1,0:T(8,128)(2,1)S(1)}, bf16[4,2,384,384]{3,2,1,0:T(8,128)(2,1)}, u32[]{:S(2)}) copy-start(bf16[4,2,384,384]{3,2,1,0:T(8,128)(2,1)} %modes.1) | copy-start | bytes 7077892
  1.8 0.7 copy-start.7
  2.5 0.7 copy-start.9
  3.2 0.7 copy-start.11
  3.9 34.0 %copy-start.8 = (s32[3,128]{1,0:T(4,128)S(1)}, s32[3,128]{1,0:T(4,128)}, u32[]{:S(2)}) copy-start(s32[3,128]{1,0:T(4,128)} %shell.3) | copy-start | bytes 4612
  3.9 50.4 %copy-start.2 = (s32[144,1]{1,0:T(8,128)S(1)}, s32[144,1]{1,0:T(8,128)}, u32[]{:S(2)}) copy-start(s32[144,1]{1,0:T(8,128)} %constant.8.clone.refs_3_) | copy-start | bytes 1732
  3.9 50.4 %copy-start.3 = (s32[16384]{0:T(1024)S(1)}, s32[16384]{0:T(1024)}, u32[]{:S(2)}) copy-start(s32[16384]{0:T(1024)} %param.18) | copy-start | bytes 196612
  3.9 50.4 %copy-start.4 = (s32[16384]{0:T(1024)S(1)}, s32[16384]{0:T(1024)}, u32[]{:S(2)}) copy-start(s32[16384]{0:T(1024)} %param.19) | copy-start | bytes 196612
  3.9 50.4 %copy-start.5 = (bf16[81,144]{1,0:T(8,128)(2,1)S(1)}, bf16[81,144]{1,0:T(8,128)(2,1)}, u32[]{:S(2)}) copy-start(bf16[81,144]{1,0:T(8,128)(2,1)} %constant.6.clone.refs_1_) | copy-start | bytes 69988
  3.9 50.4 %copy-start.6 = (bf16[144,81]{1,0:T(8,128)(2,1)S(1)}, bf16[144,81]{1,0:T(8,128)(2,1)}, u32[]{:S(2)}) copy-start(bf16[144,81]{1,0:T(8,128)(2,1)} %constant.7.clone.refs_2_) | copy-start | bytes 69988
  37.9 41.0 %copy-start.10 = (s32[3,128]{1,0:T(4,128)S(1)}, s32[3,128]{1,0:T(4,128)}, u32[]{:S(2)}) copy-start(s32[3,128]{1,0:T(4,128)} %target.1) | copy-start | bytes 4612

commit v2 on v1

--- a/solution.py
+++ b/solution.py
@@ -18,11 +18,10 @@
 F32 = jnp.float32
 BF16 = jnp.bfloat16
 HIGHEST = lax.Precision.HIGHEST
-VMEM_LIMIT = 48 * 1024 * 1024
-
-
-def params():
-    return pltpu.CompilerParams(vmem_limit_bytes=VMEM_LIMIT)
+
+
+def params(mebibytes=40):
+    return pltpu.CompilerParams(vmem_limit_bytes=mebibytes * 1024 * 1024)
 
 
 def sixteenth_cos(index):
@@ -120,7 +119,7 @@
 
 
 def pick(modes, occup, coord, atoms):
-    anywhere = pl.BlockSpec(memory_space=pl.ANY)
+    anywhere = pl.BlockSpec(memory_space=pltpu.HBM)
     return pl.pallas_call(
         pick_body,
         in_specs=[anywhere] * 4,
@@ -137,7 +136,7 @@
             pltpu.VMEM((4 * 384 * 8, LANES), F32),
             pltpu.SemaphoreType.DMA((8,)),
         ],
-        compiler_params=params(),
+        compiler_params=params(60),
     )(coord, atoms, modes, occup)
 
 
@@ -166,50 +165,79 @@
 
 
 def block_tables():
-    row = np.arange(2 * COLS)
-    column = row % COLS
-    beta, high, alpha = column // 24, (column % 24) // 3, column % 3
-    comp = 3 * alpha + beta
-    level = 8 * (row // COLS) + high
-    term = np.arange(81)
-    repeat = (term[:, None] % 9 == comp[None, :]).astype(np.float32)
-    collect = (comp[:, None] == term[None, :] // 9).astype(np.float32)
-    return repeat, collect, level.astype(np.int32)[:, None]
-
-
-def contract_body(chunk, unroll, received, repeat, collect, level, reads, writes, fc4, out, table, total):
-    for shell in range(4):
-        piece = received[:, shell, :]
-        piece = jnp.concatenate([piece, jnp.zeros((NDEV, LANES - COLS), F32)], 1)
-        low, high = shell % 2, shell // 2
-        table[low * COLS : low * COLS + COLS, high * LANES : high * LANES + LANES] = piece.T[
-            :COLS
-        ].astype(BF16)
+    column = np.arange(2 * COLS)
+    rest = column % COLS
+    comp = 3 * (rest // 24) + rest % 3
+    level = 8 * (column // COLS) + (rest % 24) // 3
+    row = np.where(comp < 8, 8 * level + comp, 128 + level)
+    place = (np.arange(2 * COLS)[:, None] == row[None, :]).astype(np.float32)
+    first, second = np.arange(81) // 9, np.arange(81) % 9
+    second = 3 * (second % 3) + second // 3
+    row = np.where(first < 8, 8 * second + first, 72 + second)
+    order = (np.arange(88)[:, None] == row[None, :]).astype(np.float32)
+    return place, order
+
+
+def two_parts(values):
+    coarse = values.astype(BF16).astype(F32)
+    return coarse, values - coarse
+
+
+def contract_body(
+    chunk, unroll, received, place, order, reads, writes, fc4, out, table, total
+):
+    for high in range(2):
+        pieces = [received[:, 2 * high + low, :] for low in range(2)]
+        parts = jnp.concatenate(two_parts(jnp.concatenate(pieces, 1)), 0).astype(BF16)
+        turned = lax.dot_general(
+            place[...].astype(BF16),
+            parts,
+            (((1,), (1,)), ((), ())),
+            preferred_element_type=F32,
+        ).astype(BF16)
+        span = pl.ds(high * LANES, LANES)
+        table[0:144, span] = turned[:, :LANES]
+        table[144:288, span] = turned[:, LANES:]
     total[...] = jnp.zeros_like(total)
-    place = lax.broadcasted_iota(jnp.int32, (2 * LANES, chunk), 0)
-
-    def split(entry):
+    level = lax.broadcasted_iota(jnp.int32, (16, chunk), 0)
+    level_pair = (level >> 3).astype(BF16)
+    level_all = level.astype(BF16)
+    low_place = lax.broadcasted_iota(jnp.int32, (2 * LANES, chunk), 0).astype(BF16)
+    unit, zero = jnp.ones((), BF16), jnp.zeros((), BF16)
+
+    def small(values):
+        return values.astype(F32).astype(BF16)
+
+    def low_hot(entry):
         low = ((entry >> 11) << 7) | (entry & 127)
-        return jnp.where(place == low, 1.0, 0.0).astype(BF16), (entry >> 7) & 15
+        return jnp.where(low_place == small(low), unit, zero)
 
     def one(step, carry):
         span = pl.ds(pl.multiple_of(step * chunk, chunk), chunk)
-        read_low, read_high = split(reads[:, span])
-        write_low, write_high = split(writes[:, span])
-        found = jnp.dot(table[...], read_low, preferred_element_type=F32)
-        found = jnp.where(level[...] == read_high, found, 0.0).astype(BF16)
-        spread = jnp.dot(repeat[...], found, preferred_element_type=F32)
-        product = fc4[:, span].astype(F32) * spread
-        coarse = product.astype(BF16)
-        fine = (product - coarse.astype(F32)).astype(BF16)
-        contrib = jnp.dot(collect[...], coarse, preferred_element_type=F32)
-        contrib = contrib + jnp.dot(collect[...], fine, preferred_element_type=F32)
-        contrib = jnp.where(level[...] == write_high, contrib, 0.0)
-        coarse = contrib.astype(BF16)
-        fine = (contrib - coarse.astype(F32)).astype(BF16)
+        coeff = jnp.dot(order[...], fc4[:, span], preferred_element_type=F32)
+        read, write = reads[:, span], writes[:, span]
+        read_high = (read >> 7) & 15
+        write_high = small((write >> 7) & 15)
+        found = jnp.dot(table[...], low_hot(read), preferred_element_type=F32)
+        found = found[:144] + found[144:]
+        main = found[0:8]
+        for high in range(1, 16):
+            main = jnp.where(read_high == high, found[8 * high : 8 * high + 8], main)
+        last = jnp.sum(jnp.where(level == read_high, found[128:144], 0.0), 0, keepdims=True)
+        contrib = coeff[64:72] * last
+        for comp in range(8):
+            contrib = contrib + coeff[8 * comp : 8 * comp + 8] * main[comp : comp + 1]
+        ninth = jnp.sum(coeff[72:80] * main, 0, keepdims=True) + coeff[80:81] * last
+        spread = []
+        for body, tail in zip(two_parts(contrib), two_parts(ninth)):
+            body = jnp.concatenate([body, body], 0).astype(BF16)
+            tail = jnp.broadcast_to(tail, level.shape).astype(BF16)
+            for pair in range(8):
+                spread.append(jnp.where(level_pair + 2 * pair == write_high, body, zero))
+            spread.append(jnp.where(level_all == write_high, tail, zero))
         total[...] += lax.dot_general(
-            jnp.concatenate([coarse, fine], 0),
-            write_low,
+            jnp.concatenate(spread, 0),
+            low_hot(write),
             (((1,), (1,)), ((), ())),
             preferred_element_type=F32,
         )
@@ -217,17 +245,17 @@
 
     lax.fori_loop(0, fc4.shape[1] // chunk, one, 0, unroll=unroll)
     for shell in range(4):
-        low, high = shell % 2, shell // 2
-        span = pl.ds(high * LANES, LANES)
-        piece = total[low * COLS : low * COLS + COLS, span]
-        piece = piece + total[(2 + low) * COLS : (2 + low) * COLS + COLS, span]
-        piece = jnp.concatenate([piece, jnp.zeros((LANES - COLS, LANES), F32)], 0)
-        out[:, shell, :] = piece.T[:, :COLS]
-
-
-def contract(received, block_in, block_out, fc4, chunk=8192, unroll=1):
+        low, span = shell % 2, pl.ds(shell // 2 * LANES, LANES)
+        body = total[64 * low : 64 * low + 64, span] + total[144 + 64 * low : 208 + 64 * low, span]
+        tail = total[128 + 8 * low : 136 + 8 * low, span] + total[272 + 8 * low : 280 + 8 * low, span]
+        rest = jnp.zeros((LANES - COLS, LANES), F32)
+        out[:, shell, :] = jnp.concatenate([body, tail, rest], 0).T[:, :COLS]
+
+
+def contract(received, block_in, block_out, fc4, chunk=16384, unroll=1):
     nblocks = fc4.shape[1]
-    repeat, collect, level = block_tables()
+    place, order = block_tables()
+    reads, writes = block_in.reshape(1, nblocks), block_out.reshape(1, nblocks)
 
     def body(*refs):
         contract_body(chunk, unroll, *refs)
@@ -236,19 +264,11 @@
         body,
         out_shape=jax.ShapeDtypeStruct((NDEV, 4, COLS), F32),
         scratch_shapes=[
-            pltpu.VMEM((2 * COLS, 2 * LANES), BF16),
+            pltpu.VMEM((4 * COLS, 2 * LANES), BF16),
             pltpu.VMEM((4 * COLS, 2 * LANES), F32),
         ],
         compiler_params=params(),
-    )(
-        received,
-        jnp.asarray(repeat, BF16),
-        jnp.asarray(collect, BF16),
-        jnp.asarray(level),
-        block_in.reshape(1, nblocks),
-        block_out.reshape(1, nblocks),
-        fc4,
-    )
+    )(received, jnp.asarray(place), jnp.asarray(order, BF16), reads, writes, fc4)
 
 
 def targets_body(received, shell, target, out):
@@ -283,23 +303,20 @@
     )(received, shell, target)
 
 
-def arrange_body(received, out, turned):
+def arrange_body(received, out):
     for comp in range(2):
         piece = received[:, comp, :]
-        piece = jnp.concatenate([piece, jnp.zeros((NDEV, LANES - COLS), F32)], 1)
-        turned[...] = piece.T
+        piece = jnp.concatenate([piece, jnp.zeros((NDEV, LANES - COLS), F32)], 1).T
         for high in range(NPH):
-            for alpha in range(3):
-                out[0, 3 * alpha : 3 * alpha + 3, comp, LANES * high : LANES * high + LANES] = turned[
-                    pl.ds(3 * high + alpha, 3, stride=24), :
-                ]
+            span = pl.ds(LANES * high, LANES)
+            out[0, 0:8, comp, span] = piece[8 * high : 8 * high + 8]
+            out[0, 8:9, comp, span] = piece[64 + high : 65 + high]
 
 
 def arrange(received):
     return pl.pallas_call(
         arrange_body,
         out_shape=jax.ShapeDtypeStruct((1, 9, 2, NPH * NDEV), F32),
-        scratch_shapes=[pltpu.VMEM((LANES, LANES), F32)],
         compiler_params=params(),
     )(received)
 

time: 95.1 us -> 90 us (0.946)
  local copies, waits for them, and re-layouts: 3.92 us -> 0.03 us
  Pallas kernels: 20.4 us -> 19.1 us
    unnamed x24 -> x14, local copies, waits for them, and re-layouts: 3.92 us -> 0.03 us
    pallas_call x1, Pallas kernels: 9.23 us -> 6.46 us  [contract(): pl.pallas_call(body, out_shape=jax.ShapeDtypeStruct((NDEV, 4, COLS), F32)...]
    pallas_call x1, Pallas kernels: 8.73 us -> 10.2 us  [pick(): pl.pallas_call(pick_body, in_specs=[anywhere] * 4, out_specs=pl.BlockSpec...]
where the time goes in v2:
time: 90 us; the launch traced here: 89.8 us
  blocking collectives  70.6 us (78%)
  Pallas kernels  19.1 us (21%)
    all_to_all x4, blocking collectives, exchange(): return lax.all_to_all(values, ALL, 0, 0, tiled=True)  70.6 us
    pallas_call x1, Pallas kernels, pick(): pl.pallas_call(pick_body, in_specs=[anywhere] * 4, out_specs=pl.BlockSpec...  10.2 us
    pallas_call x1, Pallas kernels, contract(): pl.pallas_call(body, out_shape=jax.ShapeDtypeStruct((NDEV, 4, COLS), F32)...  6.46 us

profile of v2, /device:TPU:1, one launch (start us, length us, event | category | flops | bytes accessed | tf_op | source)
XLA Modules:
  0.0 89.8 jit_solution(11732211436151069321)
XLA Ops:
  0.0 0.0 copy-start.4
  0.0 0.0 copy-start.1
  0.0 0.0 copy-start.5
  0.0 0.0 copy-start
  0.0 0.0 copy-start.3
  0.0 0.0 copy-start.2
  0.0 10.2 %shard_map.109 = f32[128,8,75]{2,1,0:T(8,128)} custom-call(s32[3,4]{1,0:T(4,128)} %coord.1, s32[2,1024]{1,0:T(2,128)} %atoms.1, bf16[4,2,384,384]{3,2,1,0:T(8,128)(2,1)} %modes.1, f32[4,384]{1,0:T(4,128)} %occup.1), custom_call_target="tpu_custom_call" | custom-call | tf_op jit(solution)/shard_map/pallas_call | solution.py:123
  10.3 25.4 %all_to_all.20.received = f32[128,8,75]{2,1,0:T(8,128)S(1)} all-to-all(f32[128,8,75]{2,1,0:T(8,128)} %shard_map.109), channel_id=1, replica_groups=mesh['grp'=4,'slab'=32] {'grp','slab'}, dimensions={0} | all-to-all | bytes 614400 | tf_op jit(solution)/shard_map/all_to_all | solution.py:325
  35.7 0.0 copy-done.5
  35.7 0.0 copy-start.6
  35.7 1.0 %shard_map.110 = f32[128,4,72]{2,1,0:T(4,128)S(1)} custom-call(f32[128,8,75]{2,1,0:T(8,128)S(1)} %all_to_all.20.received, s32[3,128]{1,0:T(4,128)S(1)} %copy-done.5), custom_call_target="tpu_custom_call" | custom-call | tf_op jit(solution)/shard_map/pallas_call | solution.py:160
  36.7 15.4 %all_to_all.21.refs_0_ = f32[128,4,72]{2,1,0:T(4,128)S(1)} all-to-all(f32[128,4,72]{2,1,0:T(4,128)S(1)} %shard_map.110), channel_id=1, replica_groups=mesh['grp'=4,'slab'=32] {'grp','slab'}, dimensions={0} | all-to-all | bytes 294912 | tf_op jit(solution)/shard_map/all_to_all | solution.py:325
  52.1 0.0 copy-done.4
  52.1 0.0 copy-done.1
  52.1 0.0 copy-done
  52.1 0.0 copy-done.3
  52.1 0.0 copy-done.2
  52.1 6.5 %shard_map.111 = f32[128,4,72]{2,1,0:T(4,128)S(1)} custom-call(f32[128,4,72]{2,1,0:T(4,128)S(1)} %all_to_all.21.refs_0_, f32[144,144]{1,0:T(8,128)S(1)} %copy-done.1, bf16[88,81]{1,0:T(8,128)(2,1)S(1)} %copy-done.4, s32[1,16384]{1,0:T(1,128)S(1)} %bitcast.3, s32[1,16384]{1,0:T(1,128)S(1)} %bitcast.4, bf16[81,16384]{1,0:T(8,128)(2,1)S(1)} %copy-done), custom_call_target="tpu_custom_call" | custom-call | tf_op jit(solution)/shard_map/pallas_call | solution.py:263
  58.6 15.4 %all_to_all.22.received = f32[128,4,72]{2,1,0:T(4,128)S(1)} all-to-all(f32[128,4,72]{2,1,0:T(4,128)S(1)} %shard_map.111), channel_id=1, replica_groups=mesh['grp'=4,'slab'=32] {'grp','slab'}, dimensions={0} | all-to-all | bytes 294912 | tf_op jit(solution)/shard_map/all_to_all | solution.py:325
  73.9 0.0 copy-done.6
  73.9 0.7 shard_map.112
  74.6 14.4 %all_to_all.23.received = f32[128,2,72]{2,1,0:T(2,128)S(1)} all-to-all(f32[128,2,72]{2,1,0:T(2,128)S(1)} %shard_map.112), channel_id=1, replica_groups=mesh['grp'=4,'slab'=32] {'grp','slab'}, dimensions={0} | all-to-all | bytes 147456 | tf_op jit(solution)/shard_map/all_to_all | solution.py:325
  89.0 0.8 shard_map.113
Async XLA Ops:
  0.0 52.1 %copy-start.4 = (bf16[88,81]{1,0:T(8,128)(2,1)S(1)}, bf16[88,81]{1,0:T(8,128)(2,1)}, u32[]{:S(2)}) copy-start(bf16[88,81]{1,0:T(8,128)(2,1)} %constant.5.clone.refs_2_) | copy-start | bytes 42772
  0.0 52.1 %copy-start.1 = (f32[144,144]{1,0:T(8,128)S(1)}, f32[144,144]{1,0:T(8,128)}, u32[]{:S(2)}) copy-start(f32[144,144]{1,0:T(8,128)} %constant.4.clone.refs_1_) | copy-start | bytes 248836
  0.0 35.7 %copy-start.5 = (s32[3,128]{1,0:T(4,128)S(1)}, s32[3,128]{1,0:T(4,128)}, u32[]{:S(2)}) copy-start(s32[3,128]{1,0:T(4,128)} %shell.3) | copy-start | bytes 4612
  0.0 52.1 %copy-start = (bf16[81,16384]{1,0:T(8,128)(2,1)S(1)}, bf16[81,16384]{1,0:T(8,128)(2,1)}, u32[]{:S(2)}) copy-start(bf16[81,16384]{1,0:T(8,128)(2,1)} %refs_5_.1) | copy-start | bytes 7962628
  0.0 52.1 %copy-start.3 = (s32[16384]{0:T(1024)S(1)}, s32[16384]{0:T(1024)}, u32[]{:S(2)}) copy-start(s32[16384]{0:T(1024)} %param.18) | copy-start | bytes 196612
  0.0 52.1 %copy-start.2 = (s32[16384]{0:T(1024)S(1)}, s32[16384]{0:T(1024)}, u32[]{:S(2)}) copy-start(s32[16384]{0:T(1024)} %param.17) | copy-start | bytes 196612
  35.7 38.2 %copy-start.6 = (s32[3,128]{1,0:T(4,128)S(1)}, s32[3,128]{1,0:T(4,128)}, u32[]{:S(2)}) copy-start(s32[3,128]{1,0:T(4,128)} %target.1) | copy-start | bytes 4612

commit v3 on v2

--- a/solution.py
+++ b/solution.py
@@ -13,6 +13,7 @@
 NDEV = 128
 NPH = 8
 COLS = 72
+PITCH = 4 * 384 + 8
 MSG = 75
 ALL = ("grp", "slab")
 F32 = jnp.float32
@@ -61,36 +62,36 @@
     copies[1].wait()
     first = pairs[0:1, :]
     second = pairs[1:2, :]
-    turn = (128 - 3 * (first & 31)) & 127
-    pairs[0:1, :] = ((first >> 5) * 3072 + second * 24) * 128 + turn
+    turn = (128 - 3 * (second & 31)) & 127
+    pairs[0:1, :] = ((second >> 5) * 384 + first * 3) * 128 + turn
     move = pltpu.make_async_copy(pairs.at[0], spots, sems.at[7])
     move.start()
     copies[0].wait()
     for q in range(4):
         loads[q].wait()
         weight = weights[q : q + 1, :]
+        real, imag = held[q, 0], held[q, 1]
+        rows[q % 2, 0:384, 0:384] = real
+        rows[q % 2, 0:384, 384:768] = imag
+        rows[q % 2, 384:768, 0:384] = imag
+        rows[q % 2, 384:768, 384:768] = -real
         for part in range(2):
-            values = held[q, part]
-            span = pl.ds(384 * part, 384)
-            scaled[:, span] = (values.astype(F32) * weight).astype(BF16)
+            values = (held[q, part].astype(F32) * weight).astype(BF16)
             for block in range(4):
-                piece = values[96 * block : 96 * block + 96]
-                rows[128 * block : 128 * block + 96, span] = piece
-                other = piece if part == 1 else -piece
-                low = 512 + 128 * block
-                rows[low : low + 96, pl.ds(384 * (1 - part), 384)] = other
+                scaled[q % 2, 128 * block : 128 * block + 96, pl.ds(384 * part, 384)] = values[
+                    96 * block : 96 * block + 96
+                ]
         for comp in range(2):
             for half in range(2):
-                start = 512 * comp + 256 * half
                 tile = lax.dot_general(
-                    scaled[...],
-                    rows[start : start + 256],
+                    rows[q % 2, 384 * comp : 384 * comp + 384],
+                    scaled[q % 2, 256 * half : 256 * half + 256],
                     (((1,), (1,)), ((), ())),
                     preferred_element_type=F32,
                 )
                 for low in range(2):
-                    base = 3072 * (2 * half + low) + 2 * q + comp
-                    dens[pl.ds(base, 384, stride=8), :] = tile[:, 128 * low : 128 * low + 128]
+                    base = PITCH * (2 * q + comp) + 384 * (2 * half + low)
+                    dens[pl.ds(base, 384), :] = tile[:, 128 * low : 128 * low + 128]
 
     lane = lax.broadcasted_iota(jnp.int32, (8, LANES), 1)
     row = lax.broadcasted_iota(jnp.int32, (8, LANES), 0)
@@ -107,15 +108,15 @@
         for high in range(NPH):
             spot = spots[high * LANES + dev]
             base = spot >> 7
-            for beta in range(3):
-                low = 24 * beta + 3 * high
-                value = dens[pl.ds(pl.multiple_of(base + 8 * beta, 8), 8), :]
+            for alpha in range(3):
+                low = 24 * alpha + 3 * high
+                value = dens[pl.ds(base + alpha, 8, stride=PITCH), :]
                 turned = pltpu.roll(value, (spot + low) & 127, 1)
                 acc = jnp.where((lane >= low) & (lane < low + 3), turned, acc)
         out[dev] = acc[:, :MSG]
         return carry
 
-    lax.fori_loop(0, NDEV, one, 0, unroll=16)
+    lax.fori_loop(0, NDEV, one, 0, unroll=64)
 
 
 def pick(modes, occup, coord, atoms):
@@ -131,9 +132,9 @@
             pltpu.VMEM((2, NPH * LANES), jnp.int32),
             pltpu.SMEM((NPH * LANES,), jnp.int32),
             pltpu.SMEM((3, 4), jnp.int32),
-            pltpu.VMEM((384, 768), BF16),
-            pltpu.VMEM((1024, 768), BF16),
-            pltpu.VMEM((4 * 384 * 8, LANES), F32),
+            pltpu.VMEM((2, 512, 768), BF16),
+            pltpu.VMEM((2, 768, 768), BF16),
+            pltpu.VMEM((PITCH * 8, LANES), F32),
             pltpu.SemaphoreType.DMA((8,)),
         ],
         compiler_params=params(60),
@@ -172,7 +173,6 @@
     row = np.where(comp < 8, 8 * level + comp, 128 + level)
     place = (np.arange(2 * COLS)[:, None] == row[None, :]).astype(np.float32)
     first, second = np.arange(81) // 9, np.arange(81) % 9
-    second = 3 * (second % 3) + second // 3
     row = np.where(first < 8, 8 * second + first, 72 + second)
     order = (np.arange(88)[:, None] == row[None, :]).astype(np.float32)
     return place, order

time: 90 us -> 88.8 us (0.987)
  Pallas kernels: 19.1 us -> 17.9 us
    pallas_call x1, Pallas kernels: 10.2 us -> 9.06 us  [pick(): pl.pallas_call(pick_body, in_specs=[anywhere] * 4, out_specs=pl.BlockSpec...]
where the time goes in v3:
time: 88.8 us; the launch traced here: 88.6 us
  blocking collectives  70.6 us (80%)
  Pallas kernels  17.9 us (20%)
    all_to_all x4, blocking collectives, exchange(): return lax.all_to_all(values, ALL, 0, 0, tiled=True)  70.6 us
    pallas_call x1, Pallas kernels, pick(): pl.pallas_call(pick_body, in_specs=[anywhere] * 4, out_specs=pl.BlockSpec...  9.06 us
    pallas_call x1, Pallas kernels, contract(): pl.pallas_call(body, out_shape=jax.ShapeDtypeStruct((NDEV, 4, COLS), F32)...  6.46 us

profile of v3, /device:TPU:1, one launch (start us, length us, event | category | flops | bytes accessed | tf_op | source)
XLA Modules:
  0.0 88.6 jit_solution(1899279485777130349)
XLA Ops:
  0.0 0.0 copy-start.4
  0.0 0.0 copy-start.1
  0.0 0.0 copy-start.5
  0.0 0.0 copy-start
  0.0 0.0 copy-start.3
  0.0 0.0 copy-start.2
  0.0 9.1 %shard_map.109 = f32[128,8,75]{2,1,0:T(8,128)} custom-call(s32[3,4]{1,0:T(4,128)} %coord.1, s32[2,1024]{1,0:T(2,128)} %atoms.1, bf16[4,2,384,384]{3,2,1,0:T(8,128)(2,1)} %modes.1, f32[4,384]{1,0:T(4,128)} %occup.1), custom_call_target="tpu_custom_call" | custom-call | tf_op jit(solution)/shard_map/pallas_call | solution.py:124
  9.1 25.4 %all_to_all.20.received = f32[128,8,75]{2,1,0:T(8,128)S(1)} all-to-all(f32[128,8,75]{2,1,0:T(8,128)} %shard_map.109), channel_id=1, replica_groups=mesh['grp'=4,'slab'=32] {'grp','slab'}, dimensions={0} | all-to-all | bytes 614400 | tf_op jit(solution)/shard_map/all_to_all | solution.py:325
  34.5 0.0 copy-done.5
  34.5 0.0 copy-start.6
  34.5 1.0 %shard_map.110 = f32[128,4,72]{2,1,0:T(4,128)S(1)} custom-call(f32[128,8,75]{2,1,0:T(8,128)S(1)} %all_to_all.20.received, s32[3,128]{1,0:T(4,128)S(1)} %copy-done.5), custom_call_target="tpu_custom_call" | custom-call | tf_op jit(solution)/shard_map/pallas_call | solution.py:161
  35.5 15.4 %all_to_all.21.refs_0_ = f32[128,4,72]{2,1,0:T(4,128)S(1)} all-to-all(f32[128,4,72]{2,1,0:T(4,128)S(1)} %shard_map.110), channel_id=1, replica_groups=mesh['grp'=4,'slab'=32] {'grp','slab'}, dimensions={0} | all-to-all | bytes 294912 | tf_op jit(solution)/shard_map/all_to_all | solution.py:325
  50.9 0.0 copy-done.4
  50.9 0.0 copy-done.1
  50.9 0.0 copy-done
  50.9 0.0 copy-done.3
  50.9 0.0 copy-done.2
  50.9 6.5 %shard_map.111 = f32[128,4,72]{2,1,0:T(4,128)S(1)} custom-call(f32[128,4,72]{2,1,0:T(4,128)S(1)} %all_to_all.21.refs_0_, f32[144,144]{1,0:T(8,128)S(1)} %copy-done.1, bf16[88,81]{1,0:T(8,128)(2,1)S(1)} %copy-done.4, s32[1,16384]{1,0:T(1,128)S(1)} %bitcast.3, s32[1,16384]{1,0:T(1,128)S(1)} %bitcast.4, bf16[81,16384]{1,0:T(8,128)(2,1)S(1)} %copy-done), custom_call_target="tpu_custom_call" | custom-call | tf_op jit(solution)/shard_map/pallas_call | solution.py:263
  57.4 15.4 %all_to_all.22.received = f32[128,4,72]{2,1,0:T(4,128)S(1)} all-to-all(f32[128,4,72]{2,1,0:T(4,128)S(1)} %shard_map.111), channel_id=1, replica_groups=mesh['grp'=4,'slab'=32] {'grp','slab'}, dimensions={0} | all-to-all | bytes 294912 | tf_op jit(solution)/shard_map/all_to_all | solution.py:325
  72.7 0.0 copy-done.6
  72.7 0.7 shard_map.112
  73.4 14.4 %all_to_all.23.received = f32[128,2,72]{2,1,0:T(2,128)S(1)} all-to-all(f32[128,2,72]{2,1,0:T(2,128)S(1)} %shard_map.112), channel_id=1, replica_groups=mesh['grp'=4,'slab'=32] {'grp','slab'}, dimensions={0} | all-to-all | bytes 147456 | tf_op jit(solution)/shard_map/all_to_all | solution.py:325
  87.8 0.8 shard_map.113
Async XLA Ops:
  0.0 50.9 %copy-start.4 = (bf16[88,81]{1,0:T(8,128)(2,1)S(1)}, bf16[88,81]{1,0:T(8,128)(2,1)}, u32[]{:S(2)}) copy-start(bf16[88,81]{1,0:T(8,128)(2,1)} %constant.5.clone.refs_2_) | copy-start | bytes 42772
  0.0 50.9 %copy-start.1 = (f32[144,144]{1,0:T(8,128)S(1)}, f32[144,144]{1,0:T(8,128)}, u32[]{:S(2)}) copy-start(f32[144,144]{1,0:T(8,128)} %constant.4.clone.refs_1_) | copy-start | bytes 248836
  0.0 34.5 %copy-start.5 = (s32[3,128]{1,0:T(4,128)S(1)}, s32[3,128]{1,0:T(4,128)}, u32[]{:S(2)}) copy-start(s32[3,128]{1,0:T(4,128)} %shell.3) | copy-start | bytes 4612
  0.0 50.9 %copy-start = (bf16[81,16384]{1,0:T(8,128)(2,1)S(1)}, bf16[81,16384]{1,0:T(8,128)(2,1)}, u32[]{:S(2)}) copy-start(bf16[81,16384]{1,0:T(8,128)(2,1)} %refs_5_.1) | copy-start | bytes 7962628
  0.0 50.9 %copy-start.3 = (s32[16384]{0:T(1024)S(1)}, s32[16384]{0:T(1024)}, u32[]{:S(2)}) copy-start(s32[16384]{0:T(1024)} %param.18) | copy-start | bytes 196612
  0.0 50.9 %copy-start.2 = (s32[16384]{0:T(1024)S(1)}, s32[16384]{0:T(1024)}, u32[]{:S(2)}) copy-start(s32[16384]{0:T(1024)} %param.17) | copy-start | bytes 196612
  34.5 38.2 %copy-start.6 = (s32[3,128]{1,0:T(4,128)S(1)}, s32[3,128]{1,0:T(4,128)}, u32[]{:S(2)}) copy-start(s32[3,128]{1,0:T(4,128)} %target.1) | copy-start | bytes 4612

commit v4 on v3

--- a/solution.py
+++ b/solution.py
@@ -14,7 +14,8 @@
 NPH = 8
 COLS = 72
 PITCH = 4 * 384 + 8
-MSG = 75
+FIRST = 5
+OTHER = 3
 ALL = ("grp", "slab")
 F32 = jnp.float32
 BF16 = jnp.bfloat16
@@ -46,7 +47,7 @@
 
 
 def pick_body(
-    coord, atoms, modes, occup, out, held, weights, pairs, spots, points, scaled, rows, dens, sems
+    coord, atoms, modes, occup, out, held, weights, pairs, spots, points, scaled, rows, dens, picked, sems
 ):
     copies = [
         pltpu.make_async_copy(occup, weights, sems.at[4]),
@@ -94,17 +95,11 @@
                     dens[pl.ds(base, 384), :] = tile[:, 128 * low : 128 * low + 128]
 
     lane = lax.broadcasted_iota(jnp.int32, (8, LANES), 1)
-    row = lax.broadcasted_iota(jnp.int32, (8, LANES), 0)
     copies[2].wait()
     move.wait()
-    start = jnp.zeros((8, LANES), F32)
-    for q in range(4):
-        for axis in range(3):
-            here = (row // 2 == q) & (lane == COLS + axis)
-            start = jnp.where(here, points[axis, q].astype(F32), start)
 
     def one(dev, carry):
-        acc = start
+        acc = jnp.zeros((8, LANES), F32)
         for high in range(NPH):
             spot = spots[high * LANES + dev]
             base = spot >> 7
@@ -113,10 +108,25 @@
                 value = dens[pl.ds(base + alpha, 8, stride=PITCH), :]
                 turned = pltpu.roll(value, (spot + low) & 127, 1)
                 acc = jnp.where((lane >= low) & (lane < low + 3), turned, acc)
-        out[dev] = acc[:, :MSG]
+        picked[pl.ds(pl.multiple_of(8 * dev, 8), 8), :] = acc
         return carry
 
     lax.fori_loop(0, NDEV, one, 0, unroll=64)
+    lane = lax.broadcasted_iota(jnp.int32, (NDEV, LANES), 1)
+    parts = [picked[pl.ds(part, NDEV, stride=8), :] for part in range(8)]
+    for part in range(4):
+        joined = jnp.where(lane < 64, parts[part], pltpu.roll(parts[part + 4], 64, 1))
+        out[pl.ds(part, NDEV, stride=FIRST), :] = joined
+    column = lax.broadcasted_iota(jnp.int32, (1, LANES), 1)
+    last = jnp.zeros((1, LANES), F32)
+    for q in range(4):
+        for axis in range(3):
+            last = jnp.where(column == 64 + 8 * q + axis, points[axis, q].astype(F32), last)
+    last = jnp.broadcast_to(last, (NDEV, LANES))
+    for part in range(8):
+        piece = pltpu.roll(parts[part], (8 * part + 64) % LANES, 1)
+        last = jnp.where((lane >= 8 * part) & (lane < 8 * part + 8), piece, last)
+    out[pl.ds(4, NDEV, stride=FIRST), :] = last
 
 
 def pick(modes, occup, coord, atoms):
@@ -125,7 +135,7 @@
         pick_body,
         in_specs=[anywhere] * 4,
         out_specs=pl.BlockSpec(memory_space=pltpu.VMEM),
-        out_shape=jax.ShapeDtypeStruct((NDEV, 8, MSG), F32),
+        out_shape=jax.ShapeDtypeStruct((NDEV * FIRST, LANES), F32),
         scratch_shapes=[
             pltpu.VMEM((4, 2, 384, 384), BF16),
             pltpu.VMEM((4, 384), F32),
@@ -135,32 +145,76 @@
             pltpu.VMEM((2, 512, 768), BF16),
             pltpu.VMEM((2, 768, 768), BF16),
             pltpu.VMEM((PITCH * 8, LANES), F32),
+            pltpu.VMEM((8 * NDEV, LANES), F32),
             pltpu.SemaphoreType.DMA((8,)),
         ],
         compiler_params=params(60),
     )(coord, atoms, modes, occup)
 
 
-def shells_body(received, shell, out):
-    values = received[...].reshape(NDEV * 8, MSG)
-    vectors = jnp.concatenate([jnp.zeros((COLS, LANES), F32), shell[...].astype(F32)], 0)
+def two_parts(values):
+    coarse = values.astype(BF16).astype(F32)
+    return coarse, values - coarse
+
+
+def split_dot(left, right):
+    left_high, left_low = [part.astype(BF16) for part in two_parts(left)]
+    right_high, right_low = [part.astype(BF16) for part in two_parts(right)]
+    total = jnp.dot(left_high, right_high, preferred_element_type=F32)
+    total = total + jnp.dot(left_high, right_low, preferred_element_type=F32)
+    return total + jnp.dot(left_low, right_high, preferred_element_type=F32)
+
+
+def pack(shells):
+    lane = lax.broadcasted_iota(jnp.int32, shells[0].shape, 1)
+    return [
+        jnp.where(lane < COLS, shells[j], pltpu.roll(shells[3], COLS - 24 * j, 1)) for j in range(3)
+    ]
+
+
+def unpack(rows):
+    lane = lax.broadcasted_iota(jnp.int32, rows[0].shape, 1)
+    turned = [pltpu.roll(rows[j], LANES - COLS + 24 * j, 1) for j in range(3)]
+    last = jnp.where(lane < 24, turned[0], jnp.where(lane < 48, turned[1], turned[2]))
+    return [*rows, last]
+
+
+def shells_body(received, shell, out, summed):
+    parts = [received[pl.ds(part, NDEV, stride=FIRST), :] for part in range(FIRST)]
+    vector = jnp.concatenate([shell[...].astype(F32), jnp.zeros((5, LANES), F32)], 0)
+    vectors = [
+        jnp.concatenate(
+            [jnp.zeros((64 + 8 * q, LANES), F32), vector, jnp.zeros((56 - 8 * q, LANES), F32)], 0
+        )
+        for q in range(4)
+    ]
     index = lax.dot_general(
-        vectors, values, (((0,), (1,)), ((), ())), preferred_element_type=F32
+        jnp.concatenate(vectors, 1),
+        parts[4],
+        (((0,), (1,)), ((), ())),
+        preferred_element_type=F32,
     )
-    lane = lax.broadcasted_iota(jnp.int32, index.shape, 1)
-    index = index + jnp.where(lane % 2 == 1, 4.0, 0.0)
-    rho = jnp.dot(sixteenth_cos(index), values, precision=HIGHEST, preferred_element_type=F32)
-    rho = rho[:, :COLS] * (1.0 / math.sqrt(512.0))
-    for slab in range(32):
-        piece = rho[4 * slab : 4 * slab + 4]
+    waves = [sixteenth_cos(index), sixteenth_cos(index + 4.0)]
+    waves = [waves[part % 2][LANES * (part // 2) : LANES * (part // 2 + 1)] for part in range(8)]
+    values = jnp.concatenate(parts[:4], 0)
+    first = split_dot(jnp.concatenate(waves[:4], 1), values)
+    second = split_dot(jnp.concatenate(waves[4:], 1), values)
+    rest = [pltpu.roll(parts[4], (LANES - 8 * part) % LANES, 1) for part in range(8)]
+    rest = split_dot(jnp.concatenate(waves, 1), jnp.concatenate(rest, 0))
+    lane = lax.broadcasted_iota(jnp.int32, (LANES, LANES), 1)
+    rho = jnp.where(lane < 64, first + pltpu.roll(second, 64, 1), pltpu.roll(rest, 64, 1))
+    summed[...] = rho * (1.0 / math.sqrt(512.0))
+    rows = pack([summed[pl.ds(low, 32, stride=4), :] for low in range(4)])
+    for j in range(3):
         for group in range(4):
-            out[32 * group + slab] = piece
+            out[pl.ds(OTHER * 32 * group + j, 32, stride=OTHER), :] = rows[j]
 
 
 def to_shells(received, shell):
     return pl.pallas_call(
         shells_body,
-        out_shape=jax.ShapeDtypeStruct((NDEV, 4, COLS), F32),
+        out_shape=jax.ShapeDtypeStruct((NDEV * OTHER, LANES), F32),
+        scratch_shapes=[pltpu.VMEM((LANES, LANES), F32)],
         compiler_params=params(),
     )(received, shell)
 
@@ -178,16 +232,12 @@
     return place, order
 
 
-def two_parts(values):
-    coarse = values.astype(BF16).astype(F32)
-    return coarse, values - coarse
-
-
 def contract_body(
     chunk, unroll, received, place, order, reads, writes, fc4, out, table, total
 ):
+    shells = unpack([received[pl.ds(j, NDEV, stride=OTHER), :] for j in range(3)])
     for high in range(2):
-        pieces = [received[:, 2 * high + low, :] for low in range(2)]
+        pieces = [shells[2 * high + low][:, :COLS] for low in range(2)]
         parts = jnp.concatenate(two_parts(jnp.concatenate(pieces, 1)), 0).astype(BF16)
         turned = lax.dot_general(
             place[...].astype(BF16),
@@ -244,12 +294,15 @@
         return carry
 
     lax.fori_loop(0, fc4.shape[1] // chunk, one, 0, unroll=unroll)
+    shells = []
     for shell in range(4):
         low, span = shell % 2, pl.ds(shell // 2 * LANES, LANES)
         body = total[64 * low : 64 * low + 64, span] + total[144 + 64 * low : 208 + 64 * low, span]
         tail = total[128 + 8 * low : 136 + 8 * low, span] + total[272 + 8 * low : 280 + 8 * low, span]
         rest = jnp.zeros((LANES - COLS, LANES), F32)
-        out[:, shell, :] = jnp.concatenate([body, tail, rest], 0).T[:, :COLS]
+        shells.append(jnp.concatenate([body, tail, rest], 0).T)
+    for j, row in enumerate(pack(shells)):
+        out[pl.ds(j, NDEV, stride=OTHER), :] = row
 
 
 def contract(received, block_in, block_out, fc4, chunk=16384, unroll=1):
@@ -262,7 +315,7 @@
 
     return pl.pallas_call(
         body,
-        out_shape=jax.ShapeDtypeStruct((NDEV, 4, COLS), F32),
+        out_shape=jax.ShapeDtypeStruct((NDEV * OTHER, LANES), F32),
         scratch_shapes=[
             pltpu.VMEM((4 * COLS, 2 * LANES), BF16),
             pltpu.VMEM((4 * COLS, 2 * LANES), F32),
@@ -273,10 +326,10 @@
 
 def targets_body(received, shell, target, out):
     rows = []
-    for low in range(4):
-        piece = received[:, low, :]
+    for j in range(3):
+        piece = received[pl.ds(j, NDEV, stride=OTHER), :]
         rows.append(piece[0:32] + piece[32:64] + piece[64:96] + piece[96:128])
-    renorm = jnp.concatenate(rows, 0)
+    renorm = jnp.concatenate(unpack(rows), 0)
     source = lax.broadcasted_iota(jnp.int32, (LANES, LANES), 0)
     order = lax.broadcasted_iota(jnp.int32, (LANES, LANES), 1)
     order = jnp.where(source == (order % 32) * 4 + order // 32, 1.0, 0.0)
@@ -287,12 +340,8 @@
     index = lax.dot_general(
         points, vectors, (((0,), (0,)), ((), ())), preferred_element_type=F32
     )
-    out[:, 0, :] = jnp.dot(
-        sixteenth_cos(index), renorm, precision=HIGHEST, preferred_element_type=F32
-    )
-    out[:, 1, :] = jnp.dot(
-        sixteenth_cos(index + 4.0), renorm, precision=HIGHEST, preferred_element_type=F32
-    )
+    out[:, 0, :] = split_dot(sixteenth_cos(index), renorm)[:, :COLS]
+    out[:, 1, :] = split_dot(sixteenth_cos(index + 4.0), renorm)[:, :COLS]
 
 
 def to_targets(received, shell, target):
@@ -322,7 +371,10 @@
 
 
 def exchange(values):
-    return lax.all_to_all(values, ALL, 0, 0, tiled=True)
+    if values.ndim == 3:
+        return lax.all_to_all(values, ALL, 0, 0, tiled=True)
+    linear = values.reshape(NDEV, 1, values.size // NDEV)
+    return lax.all_to_all(linear, ALL, 0, 0, tiled=True).reshape(values.shape)
 
 
 def shards(

time: 88.8 us -> 85.7 us (0.965)
  blocking collectives: 70.6 us -> 67.2 us
    all_to_all x4 -> x1, blocking collectives: 70.6 us -> 14.4 us  [exchange(): return lax.all_to_all(values, ALL, 0, 0, tiled=True)]
    all_to_all x0 -> x3, blocking collectives: none -> 52.9 us  [exchange(): return lax.all_to_all(linear, ALL, 0, 0, tiled=True).reshape(values.shape)]
where the time goes in v4:
time: 85.7 us; the launch traced here: 85.5 us
  blocking collectives  67.2 us (78%)
  Pallas kernels  18.2 us (21%)
    all_to_all x3, blocking collectives, exchange(): return lax.all_to_all(linear, ALL, 0, 0, tiled=True).reshape(values.shape)  52.9 us
    all_to_all x1, blocking collectives, exchange(): return lax.all_to_all(values, ALL, 0, 0, tiled=True)  14.4 us
    pallas_call x1, Pallas kernels, pick(): pl.pallas_call(pick_body, in_specs=[anywhere] * 4, out_specs=pl.BlockSpec...  9.26 us
    pallas_call x1, Pallas kernels, contract(): pl.pallas_call(body, out_shape=jax.ShapeDtypeStruct((NDEV * OTHER, LANES)...  6.48 us

profile of v4, /device:TPU:1, one launch (start us, length us, event | category | flops | bytes accessed | tf_op | source)
XLA Modules:
  0.0 85.5 jit_solution(18237955950088414322)
XLA Ops:
  0.0 0.0 copy-start.4
  0.0 0.0 copy-start.1
  0.0 0.0 copy-start.5
  0.0 0.0 copy-start
  0.0 0.0 copy-start.3
  0.0 0.0 copy-start.2
  0.0 9.3 %shard_map.109 = f32[640,128]{1,0:T(8,128)} custom-call(s32[3,4]{1,0:T(4,128)} %coord.1, s32[2,1024]{1,0:T(2,128)} %atoms.1, bf16[4,2,384,384]{3,2,1,0:T(8,128)(2,1)} %modes.1, f32[4,384]{1,0:T(4,128)} %occup.1), custom_call_target="tpu_custom_call" | custom-call | tf_op jit(solution)/shard_map/pallas_call | solution.py:134
  9.3 0.0 copy-start.6
  9.3 23.4 %all_to_all.20 = f32[128,1,640]{2,1,0:T(1,128)S(1)} all-to-all(f32[128,1,640]{2,1,0:T(1,128)} %bitcast.16), channel_id=1, replica_groups=mesh['grp'=4,'slab'=32] {'grp','slab'}, dimensions={0} | all-to-all | bytes 655360 | tf_op jit(solution)/shard_map/all_to_all | solution.py:377
  32.7 0.0 copy-done.5
  32.7 1.1 %shard_map.110 = f32[384,128]{1,0:T(8,128)S(1)} custom-call(f32[640,128]{1,0:T(8,128)S(1)} %bitcast.9, s32[3,128]{1,0:T(4,128)S(1)} %copy-done.5), custom_call_target="tpu_custom_call" | custom-call | tf_op jit(solution)/shard_map/pallas_call | solution.py:214
  33.8 14.7 %all_to_all.21 = f32[128,1,384]{2,1,0:T(1,128)S(1)} all-to-all(f32[128,1,384]{2,1,0:T(1,128)S(1)} %bitcast.10), channel_id=1, replica_groups=mesh['grp'=4,'slab'=32] {'grp','slab'}, dimensions={0} | all-to-all | bytes 393216 | tf_op jit(solution)/shard_map/all_to_all | solution.py:377
  48.6 0.0 copy-done.4
  48.6 0.0 copy-done.1
  48.6 0.0 copy-done
  48.6 0.0 copy-done.3
  48.6 0.0 copy-done.2
  48.6 6.5 %shard_map.111 = f32[384,128]{1,0:T(8,128)S(1)} custom-call(f32[384,128]{1,0:T(8,128)S(1)} %bitcast.12, f32[144,144]{1,0:T(8,128)S(1)} %copy-done.1, bf16[88,81]{1,0:T(8,128)(2,1)S(1)} %copy-done.4, s32[1,16384]{1,0:T(1,128)S(1)} %bitcast.14, s32[1,16384]{1,0:T(1,128)S(1)} %bitcast.15, bf16[81,16384]{1,0:T(8,128)(2,1)S(1)} %copy-done), custom_call_target="tpu_custom_call" | custom-call | tf_op jit(solution)/shard_map/pallas_call | solution.py:316
  55.1 14.7 %all_to_all.22 = f32[128,1,384]{2,1,0:T(1,128)S(1)} all-to-all(f32[128,1,384]{2,1,0:T(1,128)S(1)} %bitcast.13), channel_id=1, replica_groups=mesh['grp'=4,'slab'=32] {'grp','slab'}, dimensions={0} | all-to-all | bytes 393216 | tf_op jit(solution)/shard_map/all_to_all | solution.py:377
  69.8 0.0 copy-done.6
  69.8 0.5 shard_map.112
  70.4 14.4 %all_to_all.23.received = f32[128,2,72]{2,1,0:T(2,128)S(1)} all-to-all(f32[128,2,72]{2,1,0:T(2,128)S(1)} %shard_map.112), channel_id=1, replica_groups=mesh['grp'=4,'slab'=32] {'grp','slab'}, dimensions={0} | all-to-all | bytes 147456 | tf_op jit(solution)/shard_map/all_to_all | solution.py:375
  84.7 0.8 shard_map.113
Async XLA Ops:
  0.0 48.6 %copy-start.4 = (bf16[88,81]{1,0:T(8,128)(2,1)S(1)}, bf16[88,81]{1,0:T(8,128)(2,1)}, u32[]{:S(2)}) copy-start(bf16[88,81]{1,0:T(8,128)(2,1)} %constant.5.clone.refs_2_) | copy-start | bytes 42772
  0.0 48.6 %copy-start.1 = (f32[144,144]{1,0:T(8,128)S(1)}, f32[144,144]{1,0:T(8,128)}, u32[]{:S(2)}) copy-start(f32[144,144]{1,0:T(8,128)} %constant.4.clone.refs_1_) | copy-start | bytes 248836
  0.0 32.7 %copy-start.5 = (s32[3,128]{1,0:T(4,128)S(1)}, s32[3,128]{1,0:T(4,128)}, u32[]{:S(2)}) copy-start(s32[3,128]{1,0:T(4,128)} %shell.3) | copy-start | bytes 4612
  0.0 48.6 %copy-start = (bf16[81,16384]{1,0:T(8,128)(2,1)S(1)}, bf16[81,16384]{1,0:T(8,128)(2,1)}, u32[]{:S(2)}) copy-start(bf16[81,16384]{1,0:T(8,128)(2,1)} %refs_5_.1) | copy-start | bytes 7962628
  0.0 48.6 %copy-start.3 = (s32[16384]{0:T(1024)S(1)}, s32[16384]{0:T(1024)}, u32[]{:S(2)}) copy-start(s32[16384]{0:T(1024)} %param.18) | copy-start | bytes 196612
  0.0 48.6 %copy-start.2 = (s32[16384]{0:T(1024)S(1)}, s32[16384]{0:T(1024)}, u32[]{:S(2)}) copy-start(s32[16384]{0:T(1024)} %param.17) | copy-start | bytes 196612
  9.3 60.5 %copy-start.6 = (s32[3,128]{1,0:T(4,128)S(1)}, s32[3,128]{1,0:T(4,128)}, u32[]{:S(2)}) copy-start(s32[3,128]{1,0:T(4,128)} %target.1) | copy-start | bytes 4612

commit v5 on v4

--- a/solution.py
+++ b/solution.py
@@ -19,7 +19,6 @@
 ALL = ("grp", "slab")
 F32 = jnp.float32
 BF16 = jnp.bfloat16
-HIGHEST = lax.Precision.HIGHEST
 
 
 def params(mebibytes=40):
@@ -196,13 +195,13 @@
     )
     waves = [sixteenth_cos(index), sixteenth_cos(index + 4.0)]
     waves = [waves[part % 2][LANES * (part // 2) : LANES * (part // 2 + 1)] for part in range(8)]
-    values = jnp.concatenate(parts[:4], 0)
-    first = split_dot(jnp.concatenate(waves[:4], 1), values)
-    second = split_dot(jnp.concatenate(waves[4:], 1), values)
-    rest = [pltpu.roll(parts[4], (LANES - 8 * part) % LANES, 1) for part in range(8)]
-    rest = split_dot(jnp.concatenate(waves, 1), jnp.concatenate(rest, 0))
-    lane = lax.broadcasted_iota(jnp.int32, (LANES, LANES), 1)
-    rho = jnp.where(lane < 64, first + pltpu.roll(second, 64, 1), pltpu.roll(rest, 64, 1))
+    lane = lax.broadcasted_iota(jnp.int32, (NDEV, LANES), 1)
+    values = []
+    for part in range(8):
+        main = parts[part] if part < 4 else pltpu.roll(parts[part - 4], 64, 1)
+        rest = pltpu.roll(parts[4], (64 - 8 * part) % LANES, 1)
+        values.append(jnp.where(lane < 64, main, rest))
+    rho = split_dot(jnp.concatenate(waves, 1), jnp.concatenate(values, 0))
     summed[...] = rho * (1.0 / math.sqrt(512.0))
     rows = pack([summed[pl.ds(low, 32, stride=4), :] for low in range(4)])
     for j in range(3):
@@ -225,15 +224,11 @@
     comp = 3 * (rest // 24) + rest % 3
     level = 8 * (column // COLS) + (rest % 24) // 3
     row = np.where(comp < 8, 8 * level + comp, 128 + level)
-    place = (np.arange(2 * COLS)[:, None] == row[None, :]).astype(np.float32)
-    first, second = np.arange(81) // 9, np.arange(81) % 9
-    row = np.where(first < 8, 8 * second + first, 72 + second)
-    order = (np.arange(88)[:, None] == row[None, :]).astype(np.float32)
-    return place, order
+    return (np.arange(2 * COLS)[:, None] == row[None, :]).astype(np.float32)
 
 
 def contract_body(
-    chunk, unroll, received, place, order, reads, writes, fc4, out, table, total
+    chunk, unroll, received, place, reads, writes, fc4, out, table, total, terms
 ):
     shells = unpack([received[pl.ds(j, NDEV, stride=OTHER), :] for j in range(3)])
     for high in range(2):
@@ -264,7 +259,16 @@
 
     def one(step, carry):
         span = pl.ds(pl.multiple_of(step * chunk, chunk), chunk)
-        coeff = jnp.dot(order[...], fc4[:, span], preferred_element_type=F32)
+        for block in range(chunk // LANES):
+            part = pl.ds(pl.multiple_of(step * chunk + block * LANES, LANES), LANES)
+            terms[block, 0:81, :] = fc4[:, part].astype(F32)
+
+        def term(start, count, stride=1):
+            rows = pl.ds(start, count, stride=stride)
+            return jnp.concatenate(
+                [terms[block, rows, :] for block in range(chunk // LANES)], 1
+            )
+
         read, write = reads[:, span], writes[:, span]
         read_high = (read >> 7) & 15
         write_high = small((write >> 7) & 15)
@@ -274,10 +278,10 @@
         for high in range(1, 16):
             main = jnp.where(read_high == high, found[8 * high : 8 * high + 8], main)
         last = jnp.sum(jnp.where(level == read_high, found[128:144], 0.0), 0, keepdims=True)
-        contrib = coeff[64:72] * last
+        contrib = term(8, 8, 9) * last
         for comp in range(8):
-            contrib = contrib + coeff[8 * comp : 8 * comp + 8] * main[comp : comp + 1]
-        ninth = jnp.sum(coeff[72:80] * main, 0, keepdims=True) + coeff[80:81] * last
+            contrib = contrib + term(comp, 8, 9) * main[comp : comp + 1]
+        ninth = jnp.sum(term(72, 8) * main, 0, keepdims=True) + term(80, 1) * last
         spread = []
         for body, tail in zip(two_parts(contrib), two_parts(ninth)):
             body = jnp.concatenate([body, body], 0).astype(BF16)
@@ -285,29 +289,37 @@
             for pair in range(8):
                 spread.append(jnp.where(level_pair + 2 * pair == write_high, body, zero))
             spread.append(jnp.where(level_all == write_high, tail, zero))
-        total[...] += lax.dot_general(
+        added = lax.dot_general(
             jnp.concatenate(spread, 0),
             low_hot(write),
             (((1,), (1,)), ((), ())),
             preferred_element_type=F32,
         )
+        for high in range(2):
+            total[high] += added[:, high * LANES : high * LANES + LANES]
         return carry
 
     lax.fori_loop(0, fc4.shape[1] // chunk, one, 0, unroll=unroll)
     shells = []
     for shell in range(4):
-        low, span = shell % 2, pl.ds(shell // 2 * LANES, LANES)
-        body = total[64 * low : 64 * low + 64, span] + total[144 + 64 * low : 208 + 64 * low, span]
-        tail = total[128 + 8 * low : 136 + 8 * low, span] + total[272 + 8 * low : 280 + 8 * low, span]
-        rest = jnp.zeros((LANES - COLS, LANES), F32)
-        shells.append(jnp.concatenate([body, tail, rest], 0).T)
+        low, high = shell % 2, shell // 2
+        rows = []
+        for comp in range(9):
+            start = 64 * low + comp if comp < 8 else 128 + 8 * low
+            stride = 8 if comp < 8 else 1
+            rows.append(
+                total[high, pl.ds(start, 8, stride=stride), :]
+                + total[high, pl.ds(144 + start, 8, stride=stride), :]
+            )
+        rows.append(jnp.zeros((LANES - COLS, LANES), F32))
+        shells.append(jnp.concatenate(rows, 0).T)
     for j, row in enumerate(pack(shells)):
         out[pl.ds(j, NDEV, stride=OTHER), :] = row
 
 
 def contract(received, block_in, block_out, fc4, chunk=16384, unroll=1):
     nblocks = fc4.shape[1]
-    place, order = block_tables()
+    place = block_tables()
     reads, writes = block_in.reshape(1, nblocks), block_out.reshape(1, nblocks)
 
     def body(*refs):
@@ -318,10 +330,11 @@
         out_shape=jax.ShapeDtypeStruct((NDEV * OTHER, LANES), F32),
         scratch_shapes=[
             pltpu.VMEM((4 * COLS, 2 * LANES), BF16),
-            pltpu.VMEM((4 * COLS, 2 * LANES), F32),
+            pltpu.VMEM((2, 4 * COLS, LANES), F32),
+            pltpu.VMEM((chunk // LANES, 88, LANES), F32),
         ],
-        compiler_params=params(),
-    )(received, jnp.asarray(place), jnp.asarray(order, BF16), reads, writes, fc4)
+        compiler_params=params(48),
+    )(received, jnp.asarray(place), reads, writes, fc4)
 
 
 def targets_body(received, shell, target, out):
@@ -340,39 +353,35 @@
     index = lax.dot_general(
         points, vectors, (((0,), (0,)), ((), ())), preferred_element_type=F32
     )
-    out[:, 0, :] = split_dot(sixteenth_cos(index), renorm)[:, :COLS]
-    out[:, 1, :] = split_dot(sixteenth_cos(index + 4.0), renorm)[:, :COLS]
+    out[pl.ds(0, NDEV, stride=2), :] = split_dot(sixteenth_cos(index), renorm)
+    out[pl.ds(1, NDEV, stride=2), :] = split_dot(sixteenth_cos(index + 4.0), renorm)
 
 
 def to_targets(received, shell, target):
     return pl.pallas_call(
         targets_body,
-        out_shape=jax.ShapeDtypeStruct((NDEV, 2, COLS), F32),
+        out_shape=jax.ShapeDtypeStruct((NDEV * 2, LANES), F32),
         compiler_params=params(),
     )(received, shell, target)
 
 
 def arrange_body(received, out):
     for comp in range(2):
-        piece = received[:, comp, :]
-        piece = jnp.concatenate([piece, jnp.zeros((NDEV, LANES - COLS), F32)], 1).T
-        for high in range(NPH):
-            span = pl.ds(LANES * high, LANES)
-            out[0, 0:8, comp, span] = piece[8 * high : 8 * high + 8]
-            out[0, 8:9, comp, span] = piece[64 + high : 65 + high]
+        turned = received[pl.ds(comp, NDEV, stride=2), :].T
+        out[pl.ds(comp, COLS, stride=2), :] = turned[:COLS]
 
 
 def arrange(received):
-    return pl.pallas_call(
+    rows = pl.pallas_call(
         arrange_body,
-        out_shape=jax.ShapeDtypeStruct((1, 9, 2, NPH * NDEV), F32),
+        out_shape=jax.ShapeDtypeStruct((2 * COLS, LANES), F32),
         compiler_params=params(),
     )(received)
+    rows = rows.reshape(9, NPH, 2, LANES).transpose(2, 0, 1, 3)
+    return rows.reshape(1, 2, 9, NPH * LANES)
 
 
 def exchange(values):
-    if values.ndim == 3:
-        return lax.all_to_all(values, ALL, 0, 0, tiled=True)
     linear = values.reshape(NDEV, 1, values.size // NDEV)
     return lax.all_to_all(linear, ALL, 0, 0, tiled=True).reshape(values.shape)
 
@@ -384,7 +393,7 @@
     density = exchange(to_shells(picked, shell_vec))
     renorm = exchange(contract(density, block_in, block_out, fc4))
     delta = exchange(to_targets(renorm, shell_vec, target_coord))
-    return arrange(delta).transpose(0, 2, 1, 3)
+    return arrange(delta)
 
 
 def solution(mesh):

time: 85.7 us -> 84.7 us (0.988)
  Pallas kernels: 18.2 us -> 17.1 us
    all_to_all x3 -> x4, blocking collectives: 52.9 us -> 67.2 us  [exchange(): return lax.all_to_all(linear, ALL, 0, 0, tiled=True).reshape(values.shape)]
    all_to_all x1 -> x0, blocking collectives: 14.4 us -> none  [exchange(): return lax.all_to_all(values, ALL, 0, 0, tiled=True)]
where the time goes in v5:
time: 84.7 us; the launch traced here: 84.5 us
  blocking collectives  67.2 us (79%)
  Pallas kernels  17.1 us (20%)
    all_to_all x4, blocking collectives, exchange(): return lax.all_to_all(linear, ALL, 0, 0, tiled=True).reshape(values.shape)  67.2 us
    pallas_call x1, Pallas kernels, pick(): pl.pallas_call(pick_body, in_specs=[anywhere] * 4, out_specs=pl.BlockSpec...  9.24 us
    pallas_call x1, Pallas kernels, contract(): pl.pallas_call(body, out_shape=jax.ShapeDtypeStruct((NDEV * OTHER, LANES)...  5.83 us

profile of v5, /device:TPU:1, one launch (start us, length us, event | category | flops | bytes accessed | tf_op | source)
XLA Modules:
  0.0 84.5 jit_solution(15715294407579351442)
XLA Ops:
  0.0 0.0 copy-start.1
  0.0 0.0 copy-start.4
  0.0 0.0 copy-start
  0.0 0.0 copy-start.3
  0.0 0.0 copy-start.2
  0.0 9.2 %shard_map.100 = f32[640,128]{1,0:T(8,128)} custom-call(s32[3,4]{1,0:T(4,128)} %coord.1, s32[2,1024]{1,0:T(2,128)} %atoms.1, bf16[4,2,384,384]{3,2,1,0:T(8,128)(2,1)} %modes.1, f32[4,384]{1,0:T(4,128)} %occup.1), custom_call_target="tpu_custom_call" | custom-call | tf_op jit(solution)/shard_map/pallas_call | solution.py:133
  9.3 0.0 copy-start.5
  9.3 23.4 %all_to_all.20 = f32[128,1,640]{2,1,0:T(1,128)S(1)} all-to-all(f32[128,1,640]{2,1,0:T(1,128)} %bitcast.24), channel_id=1, replica_groups=mesh['grp'=4,'slab'=32] {'grp','slab'}, dimensions={0} | all-to-all | bytes 655360 | tf_op jit(solution)/shard_map/all_to_all | solution.py:386
  32.7 0.0 copy-done.4
  32.7 0.9 %shard_map.101 = f32[384,128]{1,0:T(8,128)S(1)} custom-call(f32[640,128]{1,0:T(8,128)S(1)} %bitcast.15, s32[3,128]{1,0:T(4,128)S(1)} %copy-done.4), custom_call_target="tpu_custom_call" | custom-call | tf_op jit(solution)/shard_map/pallas_call | solution.py:213
  33.6 14.7 %all_to_all.21 = f32[128,1,384]{2,1,0:T(1,128)S(1)} all-to-all(f32[128,1,384]{2,1,0:T(1,128)S(1)} %bitcast.18), channel_id=1, replica_groups=mesh['grp'=4,'slab'=32] {'grp','slab'}, dimensions={0} | all-to-all | bytes 393216 | tf_op jit(solution)/shard_map/all_to_all | solution.py:386
  48.3 0.0 copy-done.1
  48.3 0.0 copy-done
  48.3 0.0 copy-done.3
  48.3 0.0 copy-done.2
  48.3 5.8 %shard_map.102 = f32[384,128]{1,0:T(8,128)S(1)} custom-call(f32[384,128]{1,0:T(8,128)S(1)} %bitcast.16, f32[144,144]{1,0:T(8,128)S(1)} %copy-done.1, s32[1,16384]{1,0:T(1,128)S(1)} %bitcast.22, s32[1,16384]{1,0:T(1,128)S(1)} %bitcast.23, bf16[81,16384]{1,0:T(8,128)(2,1)S(1)} %copy-done), custom_call_target="tpu_custom_call" | custom-call | tf_op jit(solution)/shard_map/pallas_call | solution.py:328
  54.2 14.7 %all_to_all.22 = f32[128,1,384]{2,1,0:T(1,128)S(1)} all-to-all(f32[128,1,384]{2,1,0:T(1,128)S(1)} %bitcast.17), channel_id=1, replica_groups=mesh['grp'=4,'slab'=32] {'grp','slab'}, dimensions={0} | all-to-all | bytes 393216 | tf_op jit(solution)/shard_map/all_to_all | solution.py:386
  68.9 0.0 copy-done.5
  68.9 0.5 shard_map.103
  69.4 14.4 %all_to_all.23 = f32[128,1,256]{2,1,0:T(1,128)S(1)} all-to-all(f32[128,1,256]{2,1,0:T(1,128)S(1)} %bitcast.21), channel_id=1, replica_groups=mesh['grp'=4,'slab'=32] {'grp','slab'}, dimensions={0} | all-to-all | bytes 262144 | tf_op jit(solution)/shard_map/all_to_all | solution.py:386
  83.7 0.7 shard_map.104
Async XLA Ops:
  0.0 48.3 %copy-start.1 = (f32[144,144]{1,0:T(8,128)S(1)}, f32[144,144]{1,0:T(8,128)}, u32[]{:S(2)}) copy-start(f32[144,144]{1,0:T(8,128)} %constant.2.clone.refs_1_) | copy-start | bytes 248836
  0.0 32.7 %copy-start.4 = (s32[3,128]{1,0:T(4,128)S(1)}, s32[3,128]{1,0:T(4,128)}, u32[]{:S(2)}) copy-start(s32[3,128]{1,0:T(4,128)} %shell.3) | copy-start | bytes 4612
  0.0 48.3 %copy-start = (bf16[81,16384]{1,0:T(8,128)(2,1)S(1)}, bf16[81,16384]{1,0:T(8,128)(2,1)}, u32[]{:S(2)}) copy-start(bf16[81,16384]{1,0:T(8,128)(2,1)} %refs_4_.1) | copy-start | bytes 7962628
  0.0 48.3 %copy-start.3 = (s32[16384]{0:T(1024)S(1)}, s32[16384]{0:T(1024)}, u32[]{:S(2)}) copy-start(s32[16384]{0:T(1024)} %param.17) | copy-start | bytes 196612
  0.0 48.3 %copy-start.2 = (s32[16384]{0:T(1024)S(1)}, s32[16384]{0:T(1024)}, u32[]{:S(2)}) copy-start(s32[16384]{0:T(1024)} %param.16) | copy-start | bytes 196612
  9.3 59.6 %copy-start.5 = (s32[3,128]{1,0:T(4,128)S(1)}, s32[3,128]{1,0:T(4,128)}, u32[]{:S(2)}) copy-start(s32[3,128]{1,0:T(4,128)} %target.1) | copy-start | bytes 4612

commit v6 on v5

--- a/solution.py
+++ b/solution.py
@@ -93,7 +93,7 @@
                     base = PITCH * (2 * q + comp) + 384 * (2 * half + low)
                     dens[pl.ds(base, 384), :] = tile[:, 128 * low : 128 * low + 128]
 
-    lane = lax.broadcasted_iota(jnp.int32, (8, LANES), 1)
+    slot = lax.broadcasted_iota(jnp.int32, (8, LANES), 1) // 3
     copies[2].wait()
     move.wait()
 
@@ -106,11 +106,11 @@
                 low = 24 * alpha + 3 * high
                 value = dens[pl.ds(base + alpha, 8, stride=PITCH), :]
                 turned = pltpu.roll(value, (spot + low) & 127, 1)
-                acc = jnp.where((lane >= low) & (lane < low + 3), turned, acc)
+                acc = jnp.where(slot == low // 3, turned, acc)
         picked[pl.ds(pl.multiple_of(8 * dev, 8), 8), :] = acc
         return carry
 
-    lax.fori_loop(0, NDEV, one, 0, unroll=64)
+    lax.fori_loop(0, NDEV, one, 0, unroll=128)
     lane = lax.broadcasted_iota(jnp.int32, (NDEV, LANES), 1)
     parts = [picked[pl.ds(part, NDEV, stride=8), :] for part in range(8)]
     for part in range(4):
@@ -143,7 +143,7 @@
             pltpu.SMEM((3, 4), jnp.int32),
             pltpu.VMEM((2, 512, 768), BF16),
             pltpu.VMEM((2, 768, 768), BF16),
-            pltpu.VMEM((PITCH * 8, LANES), F32),
+            pltpu.VMEM((PITCH * 9, LANES), F32),
             pltpu.VMEM((8 * NDEV, LANES), F32),
             pltpu.SemaphoreType.DMA((8,)),
         ],

time: 84.7 us -> 84.4 us (level)
  no operation moved by 1% of the time
where the time goes in v6:
time: 84.4 us; the launch traced here: 84.1 us
  blocking collectives  67.2 us (80%)
  Pallas kernels  16.8 us (20%)
    all_to_all x4, blocking collectives, exchange(): return lax.all_to_all(linear, ALL, 0, 0, tiled=True).reshape(values.shape)  67.2 us
    pallas_call x1, Pallas kernels, pick(): pl.pallas_call(pick_body, in_specs=[anywhere] * 4, out_specs=pl.BlockSpec...  8.92 us
    pallas_call x1, Pallas kernels, contract(): pl.pallas_call(body, out_shape=jax.ShapeDtypeStruct((NDEV * OTHER, LANES)...  5.84 us

profile of v6, /device:TPU:1, one launch (start us, length us, event | category | flops | bytes accessed | tf_op | source)
XLA Modules:
  0.0 84.1 jit_solution(11732559431525100536)
XLA Ops:
  0.0 0.0 copy-start.1
  0.0 0.0 copy-start.4
  0.0 0.0 copy-start
  0.0 0.0 copy-start.3
  0.0 0.0 copy-start.2
  0.0 8.9 %shard_map.100 = f32[640,128]{1,0:T(8,128)} custom-call(s32[3,4]{1,0:T(4,128)} %coord.1, s32[2,1024]{1,0:T(2,128)} %atoms.1, bf16[4,2,384,384]{3,2,1,0:T(8,128)(2,1)} %modes.1, f32[4,384]{1,0:T(4,128)} %occup.1), custom_call_target="tpu_custom_call" | custom-call | tf_op jit(solution)/shard_map/pallas_call | solution.py:133
  9.0 0.0 copy-start.5
  9.0 23.4 %all_to_all.20 = f32[128,1,640]{2,1,0:T(1,128)S(1)} all-to-all(f32[128,1,640]{2,1,0:T(1,128)} %bitcast.24), channel_id=1, replica_groups=mesh['grp'=4,'slab'=32] {'grp','slab'}, dimensions={0} | all-to-all | bytes 655360 | tf_op jit(solution)/shard_map/all_to_all | solution.py:386
  32.4 0.0 copy-done.4
  32.4 0.9 %shard_map.101 = f32[384,128]{1,0:T(8,128)S(1)} custom-call(f32[640,128]{1,0:T(8,128)S(1)} %bitcast.15, s32[3,128]{1,0:T(4,128)S(1)} %copy-done.4), custom_call_target="tpu_custom_call" | custom-call | tf_op jit(solution)/shard_map/pallas_call | solution.py:213
  33.3 14.7 %all_to_all.21 = f32[128,1,384]{2,1,0:T(1,128)S(1)} all-to-all(f32[128,1,384]{2,1,0:T(1,128)S(1)} %bitcast.18), channel_id=1, replica_groups=mesh['grp'=4,'slab'=32] {'grp','slab'}, dimensions={0} | all-to-all | bytes 393216 | tf_op jit(solution)/shard_map/all_to_all | solution.py:386
  48.0 0.0 copy-done.1
  48.0 0.0 copy-done
  48.0 0.0 copy-done.3
  48.0 0.0 copy-done.2
  48.0 5.8 %shard_map.102 = f32[384,128]{1,0:T(8,128)S(1)} custom-call(f32[384,128]{1,0:T(8,128)S(1)} %bitcast.16, f32[144,144]{1,0:T(8,128)S(1)} %copy-done.1, s32[1,16384]{1,0:T(1,128)S(1)} %bitcast.22, s32[1,16384]{1,0:T(1,128)S(1)} %bitcast.23, bf16[81,16384]{1,0:T(8,128)(2,1)S(1)} %copy-done), custom_call_target="tpu_custom_call" | custom-call | tf_op jit(solution)/shard_map/pallas_call | solution.py:328
  53.9 14.7 %all_to_all.22 = f32[128,1,384]{2,1,0:T(1,128)S(1)} all-to-all(f32[128,1,384]{2,1,0:T(1,128)S(1)} %bitcast.17), channel_id=1, replica_groups=mesh['grp'=4,'slab'=32] {'grp','slab'}, dimensions={0} | all-to-all | bytes 393216 | tf_op jit(solution)/shard_map/all_to_all | solution.py:386
  68.6 0.0 copy-done.5
  68.6 0.5 shard_map.103
  69.1 14.4 %all_to_all.23 = f32[128,1,256]{2,1,0:T(1,128)S(1)} all-to-all(f32[128,1,256]{2,1,0:T(1,128)S(1)} %bitcast.21), channel_id=1, replica_groups=mesh['grp'=4,'slab'=32] {'grp','slab'}, dimensions={0} | all-to-all | bytes 262144 | tf_op jit(solution)/shard_map/all_to_all | solution.py:386
  83.4 0.7 shard_map.104
Async XLA Ops:
  0.0 48.0 %copy-start.1 = (f32[144,144]{1,0:T(8,128)S(1)}, f32[144,144]{1,0:T(8,128)}, u32[]{:S(2)}) copy-start(f32[144,144]{1,0:T(8,128)} %constant.2.clone.refs_1_) | copy-start | bytes 248836
  0.0 32.4 %copy-start.4 = (s32[3,128]{1,0:T(4,128)S(1)}, s32[3,128]{1,0:T(4,128)}, u32[]{:S(2)}) copy-start(s32[3,128]{1,0:T(4,128)} %shell.3) | copy-start | bytes 4612
  0.0 48.0 %copy-start = (bf16[81,16384]{1,0:T(8,128)(2,1)S(1)}, bf16[81,16384]{1,0:T(8,128)(2,1)}, u32[]{:S(2)}) copy-start(bf16[81,16384]{1,0:T(8,128)(2,1)} %refs_4_.1) | copy-start | bytes 7962628
  0.0 48.0 %copy-start.3 = (s32[16384]{0:T(1024)S(1)}, s32[16384]{0:T(1024)}, u32[]{:S(2)}) copy-start(s32[16384]{0:T(1024)} %param.17) | copy-start | bytes 196612
  0.0 48.0 %copy-start.2 = (s32[16384]{0:T(1024)S(1)}, s32[16384]{0:T(1024)}, u32[]{:S(2)}) copy-start(s32[16384]{0:T(1024)} %param.16) | copy-start | bytes 196612
  9.0 59.6 %copy-start.5 = (s32[3,128]{1,0:T(4,128)S(1)}, s32[3,128]{1,0:T(4,128)}, u32[]{:S(2)}) copy-start(s32[3,128]{1,0:T(4,128)} %target.1) | copy-start | bytes 4612

commit v7 on v6

--- a/solution.py
+++ b/solution.py
@@ -134,7 +134,7 @@
         pick_body,
         in_specs=[anywhere] * 4,
         out_specs=pl.BlockSpec(memory_space=pltpu.VMEM),
-        out_shape=jax.ShapeDtypeStruct((NDEV * FIRST, LANES), F32),
+        out_shape=pltpu.VMEM((NDEV * FIRST, LANES), F32),
         scratch_shapes=[
             pltpu.VMEM((4, 2, 384, 384), BF16),
             pltpu.VMEM((4, 384), F32),

time: 84.4 us -> 83.4 us (0.988)
  no operation moved by 1% of the time
where the time goes in v7:
time: 83.4 us; the launch traced here: 83.2 us
  blocking collectives  67 us (80%)
  Pallas kernels  16.1 us (19%)
    all_to_all x4, blocking collectives, exchange(): return lax.all_to_all(linear, ALL, 0, 0, tiled=True).reshape(values.shape)  67 us
    pallas_call x1, Pallas kernels, pick(): pl.pallas_call(pick_body, in_specs=[anywhere] * 4, out_specs=pl.BlockSpec...  8.2 us
    pallas_call x1, Pallas kernels, contract(): pl.pallas_call(body, out_shape=jax.ShapeDtypeStruct((NDEV * OTHER, LANES)...  5.83 us

profile of v7, /device:TPU:1, one launch (start us, length us, event | category | flops | bytes accessed | tf_op | source)
XLA Modules:
  0.0 83.2 jit_solution(1166287307905390903)
XLA Ops:
  0.0 0.0 copy-start.1
  0.0 0.0 copy-start.4
  0.0 0.0 copy-start
  0.0 0.0 copy-start.3
  0.0 0.0 copy-start.2
  0.0 8.2 %shard_map.100 = f32[640,128]{1,0:T(8,128)S(1)} custom-call(s32[3,4]{1,0:T(4,128)} %coord.1, s32[2,1024]{1,0:T(2,128)} %atoms.1, bf16[4,2,384,384]{3,2,1,0:T(8,128)(2,1)} %modes.1, f32[4,384]{1,0:T(4,128)} %occup.1), custom_call_target="tpu_custom_call" | custom-call | tf_op jit(solution)/shard_map/pallas_call | solution.py:133
  8.2 0.0 copy-start.5
  8.3 23.2 %all_to_all.20 = f32[128,1,640]{2,1,0:T(1,128)S(1)} all-to-all(f32[128,1,640]{2,1,0:T(1,128)S(1)} %bitcast.16), channel_id=1, replica_groups=mesh['grp'=4,'slab'=32] {'grp','slab'}, dimensions={0} | all-to-all | bytes 655360 | tf_op jit(solution)/shard_map/all_to_all | solution.py:386
  31.5 0.0 copy-done.4
  31.5 0.9 %shard_map.101 = f32[384,128]{1,0:T(8,128)S(1)} custom-call(f32[640,128]{1,0:T(8,128)S(1)} %bitcast.15, s32[3,128]{1,0:T(4,128)S(1)} %copy-done.4), custom_call_target="tpu_custom_call" | custom-call | tf_op jit(solution)/shard_map/pallas_call | solution.py:213
  32.3 14.7 %all_to_all.21 = f32[128,1,384]{2,1,0:T(1,128)S(1)} all-to-all(f32[128,1,384]{2,1,0:T(1,128)S(1)} %bitcast.19), channel_id=1, replica_groups=mesh['grp'=4,'slab'=32] {'grp','slab'}, dimensions={0} | all-to-all | bytes 393216 | tf_op jit(solution)/shard_map/all_to_all | solution.py:386
  47.1 0.0 copy-done.1
  47.1 0.0 copy-done
  47.1 0.0 copy-done.3
  47.1 0.0 copy-done.2
  47.1 5.8 %shard_map.102 = f32[384,128]{1,0:T(8,128)S(1)} custom-call(f32[384,128]{1,0:T(8,128)S(1)} %bitcast.17, f32[144,144]{1,0:T(8,128)S(1)} %copy-done.1, s32[1,16384]{1,0:T(1,128)S(1)} %bitcast.23, s32[1,16384]{1,0:T(1,128)S(1)} %bitcast.24, bf16[81,16384]{1,0:T(8,128)(2,1)S(1)} %copy-done), custom_call_target="tpu_custom_call" | custom-call | tf_op jit(solution)/shard_map/pallas_call | solution.py:328
  52.9 14.7 %all_to_all.22 = f32[128,1,384]{2,1,0:T(1,128)S(1)} all-to-all(f32[128,1,384]{2,1,0:T(1,128)S(1)} %bitcast.18), channel_id=1, replica_groups=mesh['grp'=4,'slab'=32] {'grp','slab'}, dimensions={0} | all-to-all | bytes 393216 | tf_op jit(solution)/shard_map/all_to_all | solution.py:386
  67.6 0.0 copy-done.5
  67.6 0.5 shard_map.103
  68.1 14.4 %all_to_all.23 = f32[128,1,256]{2,1,0:T(1,128)S(1)} all-to-all(f32[128,1,256]{2,1,0:T(1,128)S(1)} %bitcast.22), channel_id=1, replica_groups=mesh['grp'=4,'slab'=32] {'grp','slab'}, dimensions={0} | all-to-all | bytes 262144 | tf_op jit(solution)/shard_map/all_to_all | solution.py:386
  82.5 0.7 shard_map.104
Async XLA Ops:
  0.0 47.1 %copy-start.1 = (f32[144,144]{1,0:T(8,128)S(1)}, f32[144,144]{1,0:T(8,128)}, u32[]{:S(2)}) copy-start(f32[144,144]{1,0:T(8,128)} %constant.2.clone.refs_1_) | copy-start | bytes 248836
  0.0 31.5 %copy-start.4 = (s32[3,128]{1,0:T(4,128)S(1)}, s32[3,128]{1,0:T(4,128)}, u32[]{:S(2)}) copy-start(s32[3,128]{1,0:T(4,128)} %shell.3) | copy-start | bytes 4612
  0.0 47.1 %copy-start = (bf16[81,16384]{1,0:T(8,128)(2,1)S(1)}, bf16[81,16384]{1,0:T(8,128)(2,1)}, u32[]{:S(2)}) copy-start(bf16[81,16384]{1,0:T(8,128)(2,1)} %refs_4_.1) | copy-start | bytes 7962628
  0.0 47.1 %copy-start.3 = (s32[16384]{0:T(1024)S(1)}, s32[16384]{0:T(1024)}, u32[]{:S(2)}) copy-start(s32[16384]{0:T(1024)} %param.17) | copy-start | bytes 196612
  0.0 47.1 %copy-start.2 = (s32[16384]{0:T(1024)S(1)}, s32[16384]{0:T(1024)}, u32[]{:S(2)}) copy-start(s32[16384]{0:T(1024)} %param.16) | copy-start | bytes 196612
  8.2 59.4 %copy-start.5 = (s32[3,128]{1,0:T(4,128)S(1)}, s32[3,128]{1,0:T(4,128)}, u32[]{:S(2)}) copy-start(s32[3,128]{1,0:T(4,128)} %target.1) | copy-start | bytes 4612

commit v8 on v7

--- a/solution.py
+++ b/solution.py
@@ -54,11 +54,8 @@
         pltpu.make_async_copy(coord, points, sems.at[6]),
     ]
     loads = [pltpu.make_async_copy(modes.at[q], held.at[q], sems.at[q]) for q in range(4)]
-    loads[0].start()
-    for copy in copies:
+    for copy in copies + loads:
         copy.start()
-    for load in loads[1:]:
-        load.start()
     copies[1].wait()
     first = pairs[0:1, :]
     second = pairs[1:2, :]
@@ -241,8 +238,8 @@
             preferred_element_type=F32,
         ).astype(BF16)
         span = pl.ds(high * LANES, LANES)
-        table[0:144, span] = turned[:, :LANES]
-        table[144:288, span] = turned[:, LANES:]
+        table[:, span] = turned[:, :LANES]
+        table[:, pl.ds((2 + high) * LANES, LANES)] = turned[:, LANES:]
     total[...] = jnp.zeros_like(total)
     level = lax.broadcasted_iota(jnp.int32, (16, chunk), 0)
     level_pair = (level >> 3).astype(BF16)
@@ -272,8 +269,9 @@
         read, write = reads[:, span], writes[:, span]
         read_high = (read >> 7) & 15
         write_high = small((write >> 7) & 15)
-        found = jnp.dot(table[...], low_hot(read), preferred_element_type=F32)
-        found = found[:144] + found[144:]
+        hot = low_hot(read)
+        hot = jnp.concatenate([hot, hot], 0)
+        found = jnp.dot(table[...], hot, preferred_element_type=F32)
         main = found[0:8]
         for high in range(1, 16):
             main = jnp.where(read_high == high, found[8 * high : 8 * high + 8], main)
@@ -329,7 +327,7 @@
         body,
         out_shape=jax.ShapeDtypeStruct((NDEV * OTHER, LANES), F32),
         scratch_shapes=[
-            pltpu.VMEM((4 * COLS, 2 * LANES), BF16),
+            pltpu.VMEM((2 * COLS, 4 * LANES), BF16),
             pltpu.VMEM((2, 4 * COLS, LANES), F32),
             pltpu.VMEM((chunk // LANES, 88, LANES), F32),
         ],

time: 83.4 us -> 83.4 us (level)
  no operation moved by 1% of the time
where the time goes in v8:
time: 83.4 us; the launch traced here: 83.2 us
  blocking collectives  67 us (80%)
  Pallas kernels  16.1 us (19%)
    all_to_all x4, blocking collectives, exchange(): return lax.all_to_all(linear, ALL, 0, 0, tiled=True).reshape(values.shape)  67 us
    pallas_call x1, Pallas kernels, pick(): pl.pallas_call(pick_body, in_specs=[anywhere] * 4, out_specs=pl.BlockSpec...  8.24 us
    pallas_call x1, Pallas kernels, contract(): pl.pallas_call(body, out_shape=jax.ShapeDtypeStruct((NDEV * OTHER, LANES)...  5.78 us

profile of v8, /device:TPU:1, one launch (start us, length us, event | category | flops | bytes accessed | tf_op | source)
XLA Modules:
  0.0 83.2 jit_solution(12412362741453152262)
XLA Ops:
  0.0 0.0 copy-start.1
  0.0 0.0 copy-start.4
  0.0 0.0 copy-start
  0.0 0.0 copy-start.3
  0.0 0.0 copy-start.2
  0.0 8.2 %shard_map.100 = f32[640,128]{1,0:T(8,128)S(1)} custom-call(s32[3,4]{1,0:T(4,128)} %coord.1, s32[2,1024]{1,0:T(2,128)} %atoms.1, bf16[4,2,384,384]{3,2,1,0:T(8,128)(2,1)} %modes.1, f32[4,384]{1,0:T(4,128)} %occup.1), custom_call_target="tpu_custom_call" | custom-call | tf_op jit(solution)/shard_map/pallas_call | solution.py:130
  8.3 0.0 copy-start.5
  8.3 23.2 %all_to_all.20 = f32[128,1,640]{2,1,0:T(1,128)S(1)} all-to-all(f32[128,1,640]{2,1,0:T(1,128)S(1)} %bitcast.16), channel_id=1, replica_groups=mesh['grp'=4,'slab'=32] {'grp','slab'}, dimensions={0} | all-to-all | bytes 655360 | tf_op jit(solution)/shard_map/all_to_all | solution.py:384
  31.5 0.0 copy-done.4
  31.5 0.9 %shard_map.101 = f32[384,128]{1,0:T(8,128)S(1)} custom-call(f32[640,128]{1,0:T(8,128)S(1)} %bitcast.15, s32[3,128]{1,0:T(4,128)S(1)} %copy-done.4), custom_call_target="tpu_custom_call" | custom-call | tf_op jit(solution)/shard_map/pallas_call | solution.py:210
  32.4 14.7 %all_to_all.21 = f32[128,1,384]{2,1,0:T(1,128)S(1)} all-to-all(f32[128,1,384]{2,1,0:T(1,128)S(1)} %bitcast.19), channel_id=1, replica_groups=mesh['grp'=4,'slab'=32] {'grp','slab'}, dimensions={0} | all-to-all | bytes 393216 | tf_op jit(solution)/shard_map/all_to_all | solution.py:384
  47.1 0.0 copy-done.1
  47.1 0.0 copy-done
  47.1 0.0 copy-done.3
  47.1 0.0 copy-done.2
  47.1 5.8 %shard_map.102 = f32[384,128]{1,0:T(8,128)S(1)} custom-call(f32[384,128]{1,0:T(8,128)S(1)} %bitcast.17, f32[144,144]{1,0:T(8,128)S(1)} %copy-done.1, s32[1,16384]{1,0:T(1,128)S(1)} %bitcast.23, s32[1,16384]{1,0:T(1,128)S(1)} %bitcast.24, bf16[81,16384]{1,0:T(8,128)(2,1)S(1)} %copy-done), custom_call_target="tpu_custom_call" | custom-call | tf_op jit(solution)/shard_map/pallas_call | solution.py:326
  52.9 14.7 %all_to_all.22 = f32[128,1,384]{2,1,0:T(1,128)S(1)} all-to-all(f32[128,1,384]{2,1,0:T(1,128)S(1)} %bitcast.18), channel_id=1, replica_groups=mesh['grp'=4,'slab'=32] {'grp','slab'}, dimensions={0} | all-to-all | bytes 393216 | tf_op jit(solution)/shard_map/all_to_all | solution.py:384
  67.6 0.0 copy-done.5
  67.6 0.5 shard_map.103
  68.1 14.4 %all_to_all.23 = f32[128,1,256]{2,1,0:T(1,128)S(1)} all-to-all(f32[128,1,256]{2,1,0:T(1,128)S(1)} %bitcast.22), channel_id=1, replica_groups=mesh['grp'=4,'slab'=32] {'grp','slab'}, dimensions={0} | all-to-all | bytes 262144 | tf_op jit(solution)/shard_map/all_to_all | solution.py:384
  82.5 0.7 shard_map.104
Async XLA Ops:
  0.0 47.1 %copy-start.1 = (f32[144,144]{1,0:T(8,128)S(1)}, f32[144,144]{1,0:T(8,128)}, u32[]{:S(2)}) copy-start(f32[144,144]{1,0:T(8,128)} %constant.2.clone.refs_1_) | copy-start | bytes 248836
  0.0 31.5 %copy-start.4 = (s32[3,128]{1,0:T(4,128)S(1)}, s32[3,128]{1,0:T(4,128)}, u32[]{:S(2)}) copy-start(s32[3,128]{1,0:T(4,128)} %shell.3) | copy-start | bytes 4612
  0.0 47.1 %copy-start = (bf16[81,16384]{1,0:T(8,128)(2,1)S(1)}, bf16[81,16384]{1,0:T(8,128)(2,1)}, u32[]{:S(2)}) copy-start(bf16[81,16384]{1,0:T(8,128)(2,1)} %refs_4_.1) | copy-start | bytes 7962628
  0.0 47.1 %copy-start.3 = (s32[16384]{0:T(1024)S(1)}, s32[16384]{0:T(1024)}, u32[]{:S(2)}) copy-start(s32[16384]{0:T(1024)} %param.17) | copy-start | bytes 196612
  0.0 47.1 %copy-start.2 = (s32[16384]{0:T(1024)S(1)}, s32[16384]{0:T(1024)}, u32[]{:S(2)}) copy-start(s32[16384]{0:T(1024)} %param.16) | copy-start | bytes 196612
  8.3 59.3 %copy-start.5 = (s32[3,128]{1,0:T(4,128)S(1)}, s32[3,128]{1,0:T(4,128)}, u32[]{:S(2)}) copy-start(s32[3,128]{1,0:T(4,128)} %target.1) | copy-start | bytes 4612
